TPU v7x, 256 devices: a whole 4x4x8 slice. The times are simulated.
256 devices in a mesh: segment: 8 (over z), neuron: 32 (over x, y, core).
Axes of the slice: x: 4, y: 4, z: 8, core: 2. Of those that a mesh axis runs over, the one named last changes fastest.
Arguments:
- samples: bfloat16 [4, 128, 65536], P(None, None, 'neuron'), may hold values from -48 to 48
- weights: bfloat16 [16, 65536, 256], P('segment', 'neuron'), may hold values from -0.5 to 0.5
- biases: bfloat16 [16, 65536], P('segment', 'neuron'), may hold values from -12 to 12
- near_blocks: int32 [16, 1024, 3], P('segment', 'neuron'), may hold values from 0 to 31
- remote_cols: int32 [16, 1024], P('segment'), may hold values from 0 to 1023, as said below
Outputs:
- activations: bfloat16 [4, 128, 65536], P(None, 'segment', 'neuron')
Inputs may be any that keep to these rules, and one draw needn't show every extreme that they name: In every layer, the 32 output blocks of one index of neuron (blocks 32 p to 32 p + 31) name remote columns whose owner remote_cols // 32 is named by exactly 0 or exactly 2 of those blocks.
All inputs are finite; a program needn't handle non-finite values.
Results may differ from a plain program's by a relative error of at most 0.028.
Values may be sent and summed in bfloat16 or wider, within the bound.
A program may use at most 128 MiB of HBM per device.

v0:
```python
import jax
import jax.numpy as jnp
from jax import lax
from jax.sharding import PartitionSpec as P


def from_behind(value, axis, steps):
    count = lax.axis_size(axis)
    leading, last = (max(0, -steps), min(count, count - steps))
    return lax.ppermute(value, axis, [(source, source + steps) for source in range(leading, last)])


def slot_tables(cols, owners_count, per_dev, capacity, me_index):
    owner = cols // per_dev
    onehot = (owner[:, None] == jnp.arange(owners_count, dtype=jnp.int32)[None, :]).astype(
        jnp.int32
    )
    grouped = onehot.reshape(owners_count, per_dev, owners_count)
    before = jnp.cumsum(grouped, axis=1) - grouped
    rank = jnp.sum(before * grouped, axis=2).reshape(-1)
    asker = jnp.arange(cols.shape[0], dtype=jnp.int32) // per_dev
    target = jnp.where(owner == me_index, asker * capacity + rank, owners_count * capacity)
    send_index = (
        jnp.zeros((owners_count * capacity,), jnp.int32).at[target].set(cols % per_dev, mode="drop")
    )
    mine_owner = lax.dynamic_slice_in_dim(owner, me_index * per_dev, per_dev)
    mine_rank = lax.dynamic_slice_in_dim(rank, me_index * per_dev, per_dev)
    return (send_index, mine_owner * capacity + mine_rank)


def run_layer(act, weight, bias, near, cols, owners_count, capacity, me_index):
    width, rows = act.shape
    per_dev = width // 64
    blocks = act.reshape(per_dev, 64, rows)
    shaped = weight.reshape(per_dev, 64, weight.shape[1])
    near_width = near.shape[1] * 64
    near_taken = jnp.take(blocks, near.reshape(-1), axis=0).reshape(per_dev, near_width, rows)
    send_index, recv_index = slot_tables(cols, owners_count, per_dev, capacity, me_index)
    outgoing = jnp.take(blocks, send_index, axis=0).reshape(owners_count * capacity * 64, rows)
    incoming = lax.all_to_all(outgoing, "neuron", split_axis=0, concat_axis=0, tiled=True)
    far_taken = jnp.take(incoming.reshape(owners_count * capacity, 64, rows), recv_index, axis=0)
    joined = jnp.concatenate([near_taken, far_taken], axis=1)
    total = jnp.einsum("bok,bkr->bor", shaped, joined, preferred_element_type=jnp.float32)
    total = total.reshape(width, rows) + bias.astype(jnp.float32)[:, None]
    return jnp.clip(total, 0.0, 32.0).astype(jnp.bfloat16)


def local(samples, weights, biases, near_blocks, remote_cols):
    batches, rows, width = samples.shape
    sections = lax.axis_size("segment")
    owners_count = lax.axis_size("neuron")
    per_dev = width // 64
    capacity = 2 * max(1, per_dev // owners_count)
    segment_index = lax.axis_index("segment")
    me_index = lax.axis_index("neuron")
    layer_count = weights.shape[0]
    total_steps = batches + sections - 1

    def one_step(step, carry):
        held, gathered = carry
        fresh = lax.dynamic_index_in_dim(samples, jnp.clip(step, 0, batches - 1), 0, keepdims=False)
        current = jnp.where(segment_index == 0, fresh.T, held)
        for layer in range(layer_count):
            current = run_layer(
                current,
                weights[layer],
                biases[layer],
                near_blocks[layer],
                remote_cols[layer],
                owners_count,
                capacity,
                me_index,
            )
        finished = step - (sections - 1)
        keep = (segment_index == sections - 1) & (finished >= 0)
        updated = lax.dynamic_update_index_in_dim(
            gathered, current.T, jnp.clip(finished, 0, batches - 1), 0
        )
        gathered = jnp.where(keep, updated, gathered)
        held = from_behind(current, "segment", 1)
        return (held, gathered)

    start_carry = (
        jnp.zeros((width, rows), jnp.bfloat16),
        jnp.zeros((batches, rows, width), jnp.bfloat16),
    )
    _, gathered = lax.fori_loop(0, total_steps, one_step, start_carry)
    shares = lax.psum_scatter(gathered, "segment", scatter_dimension=1, tiled=True).astype(
        jnp.float32
    )
    return shares.astype(jnp.bfloat16)


def solution(mesh):
    return jax.shard_map(
        local,
        mesh=mesh,
        in_specs=(
            P(None, None, "neuron"),
            P("segment", "neuron", None),
            P("segment", "neuron"),
            P("segment", "neuron", None),
            P("segment", None),
        ),
        out_specs=P(None, "segment", "neuron"),
        check_vma=False,
    )
```

profile of v0, /device:TPU:1, one launch (start us, length us, event | category | flops | bytes accessed | tf_op | source)
XLA Modules:
  0.0 942.6 jit_solution(11806926135122695486)
XLA Ops:
  9.8 882.1 %while.20 = (s32[]{:T(128)}, bf16[2048,128]{1,0:T(8,128)(2,1)S(1)}, bf16[4,128,2048]{2,1,0:T(8,128)(2,1)}, pred[]{:T(512)}, bf16[4,128,2048]{2,1,0:T(8,128)(2,1)...) while((s32[]{:T(128)}, bf16[2048,128]{1,0:T(8,128)(2,1)S(1)}, ...), condition=%wide.region_7.11_spmd, body=%wide.region_0.10_spmd.sunk | while | flops 284612928 | bytes 81658168 | solution.py:87
  23.9 8.6 all-to-all-start
  42.0 7.5 all-to-all-done
  61.2 13.5 %all-to-all-done.1 = bf16[32,128,128]{2,1,0:T(8,128)(2,1)S(1)} async-done(((bf16[32,128,128]{2,1,0:T(8,128)(2,1)}), bf16[32,128,128]{2,1,0:T(8,128)(2,1)S(1)}, u32[]{:S(2)}, u32[]{:S(2)}) %all-to-all-start.1) | async-done | bytes 1048608 | tf_op jit(solution)/shard_map/while/body/eval_jaxpr/all_to_all | solution.py:40
  82.3 10.1 %collective-permute-done = bf16[2048,128]{1,0:T(8,128)(2,1)S(1)} collective-permute-done((bf16[2048,128]{1,0:T(8,128)(2,1)S(1)}, bf16[2048,128]{1,0:T(8,128)(2,1)S(1)}, u32[]{:S(2)}, u32[]{:S(2)}) %collective-permute-start) | collective-permute-done | bytes 524320 | tf_op jit(solution)/shard_map/while/body/eval_jaxpr/ppermute | solution.py:10
  106.5 4.5 all-to-all-start
  120.5 7.6 all-to-all-done
  139.8 13.5 %all-to-all-done.1 = bf16[32,128,128]{2,1,0:T(8,128)(2,1)S(1)} async-done(((bf16[32,128,128]{2,1,0:T(8,128)(2,1)}), bf16[32,128,128]{2,1,0:T(8,128)(2,1)S(1)}, u32[]{:S(2)}, u32[]{:S(2)}) %all-to-all-start.1) | async-done | bytes 1048608 | tf_op jit(solution)/shard_map/while/body/eval_jaxpr/all_to_all | solution.py:40
  161.5 10.1 %collective-permute-done = bf16[2048,128]{1,0:T(8,128)(2,1)S(1)} collective-permute-done((bf16[2048,128]{1,0:T(8,128)(2,1)S(1)}, bf16[2048,128]{1,0:T(8,128)(2,1)S(1)}, u32[]{:S(2)}, u32[]{:S(2)}) %collective-permute-start) | collective-permute-done | bytes 524320 | tf_op jit(solution)/shard_map/while/body/eval_jaxpr/ppermute | solution.py:10
  185.6 4.5 all-to-all-start
  199.6 7.6 all-to-all-done
  218.9 13.5 %all-to-all-done.1 = bf16[32,128,128]{2,1,0:T(8,128)(2,1)S(1)} async-done(((bf16[32,128,128]{2,1,0:T(8,128)(2,1)}), bf16[32,128,128]{2,1,0:T(8,128)(2,1)S(1)}, u32[]{:S(2)}, u32[]{:S(2)}) %all-to-all-start.1) | async-done | bytes 1048608 | tf_op jit(solution)/shard_map/while/body/eval_jaxpr/all_to_all | solution.py:40
  240.6 10.1 %collective-permute-done = bf16[2048,128]{1,0:T(8,128)(2,1)S(1)} collective-permute-done((bf16[2048,128]{1,0:T(8,128)(2,1)S(1)}, bf16[2048,128]{1,0:T(8,128)(2,1)S(1)}, u32[]{:S(2)}, u32[]{:S(2)}) %collective-permute-start) | collective-permute-done | bytes 524320 | tf_op jit(solution)/shard_map/while/body/eval_jaxpr/ppermute | solution.py:10
  264.8 4.5 all-to-all-start
  278.8 7.6 all-to-all-done
  298.1 13.5 %all-to-all-done.1 = bf16[32,128,128]{2,1,0:T(8,128)(2,1)S(1)} async-done(((bf16[32,128,128]{2,1,0:T(8,128)(2,1)}), bf16[32,128,128]{2,1,0:T(8,128)(2,1)S(1)}, u32[]{:S(2)}, u32[]{:S(2)}) %all-to-all-start.1) | async-done | bytes 1048608 | tf_op jit(solution)/shard_map/while/body/eval_jaxpr/all_to_all | solution.py:40
  319.8 10.1 %collective-permute-done = bf16[2048,128]{1,0:T(8,128)(2,1)S(1)} collective-permute-done((bf16[2048,128]{1,0:T(8,128)(2,1)S(1)}, bf16[2048,128]{1,0:T(8,128)(2,1)S(1)}, u32[]{:S(2)}, u32[]{:S(2)}) %collective-permute-start) | collective-permute-done | bytes 524320 | tf_op jit(solution)/shard_map/while/body/eval_jaxpr/ppermute | solution.py:10
  357.9 7.6 all-to-all-done
  377.2 13.5 %all-to-all-done.1 = bf16[32,128,128]{2,1,0:T(8,128)(2,1)S(1)} async-done(((bf16[32,128,128]{2,1,0:T(8,128)(2,1)}), bf16[32,128,128]{2,1,0:T(8,128)(2,1)S(1)}, u32[]{:S(2)}, u32[]{:S(2)}) %all-to-all-start.1) | async-done | bytes 1048608 | tf_op jit(solution)/shard_map/while/body/eval_jaxpr/all_to_all | solution.py:40
  393.7 4.9 collective-permute-start
  399.6 10.1 %collective-permute-done = bf16[2048,128]{1,0:T(8,128)(2,1)S(1)} collective-permute-done((bf16[2048,128]{1,0:T(8,128)(2,1)S(1)}, bf16[2048,128]{1,0:T(8,128)(2,1)S(1)}, u32[]{:S(2)}, u32[]{:S(2)}) %collective-permute-start) | collective-permute-done | bytes 524320 | tf_op jit(solution)/shard_map/while/body/eval_jaxpr/ppermute | solution.py:10
  423.8 4.5 all-to-all-start
  437.8 7.6 all-to-all-done
  457.1 13.5 %all-to-all-done.1 = bf16[32,128,128]{2,1,0:T(8,128)(2,1)S(1)} async-done(((bf16[32,128,128]{2,1,0:T(8,128)(2,1)}), bf16[32,128,128]{2,1,0:T(8,128)(2,1)S(1)}, u32[]{:S(2)}, u32[]{:S(2)}) %all-to-all-start.1) | async-done | bytes 1048608 | tf_op jit(solution)/shard_map/while/body/eval_jaxpr/all_to_all | solution.py:40
  473.6 5.3 collective-permute-start
  480.0 10.1 %collective-permute-done = bf16[2048,128]{1,0:T(8,128)(2,1)S(1)} collective-permute-done((bf16[2048,128]{1,0:T(8,128)(2,1)S(1)}, bf16[2048,128]{1,0:T(8,128)(2,1)S(1)}, u32[]{:S(2)}, u32[]{:S(2)}) %collective-permute-start) | collective-permute-done | bytes 524320 | tf_op jit(solution)/shard_map/while/body/eval_jaxpr/ppermute | solution.py:10
  518.1 7.6 all-to-all-done
  537.5 13.5 %all-to-all-done.1 = bf16[32,128,128]{2,1,0:T(8,128)(2,1)S(1)} async-done(((bf16[32,128,128]{2,1,0:T(8,128)(2,1)}), bf16[32,128,128]{2,1,0:T(8,128)(2,1)S(1)}, u32[]{:S(2)}, u32[]{:S(2)}) %all-to-all-start.1) | async-done | bytes 1048608 | tf_op jit(solution)/shard_map/while/body/eval_jaxpr/all_to_all | solution.py:40
  553.9 5.4 collective-permute-start
  560.4 10.1 %collective-permute-done = bf16[2048,128]{1,0:T(8,128)(2,1)S(1)} collective-permute-done((bf16[2048,128]{1,0:T(8,128)(2,1)S(1)}, bf16[2048,128]{1,0:T(8,128)(2,1)S(1)}, u32[]{:S(2)}, u32[]{:S(2)}) %collective-permute-start) | collective-permute-done | bytes 524320 | tf_op jit(solution)/shard_map/while/body/eval_jaxpr/ppermute | solution.py:10
  584.5 4.5 all-to-all-start
  598.5 7.6 all-to-all-done
  617.8 13.5 %all-to-all-done.1 = bf16[32,128,128]{2,1,0:T(8,128)(2,1)S(1)} async-done(((bf16[32,128,128]{2,1,0:T(8,128)(2,1)}), bf16[32,128,128]{2,1,0:T(8,128)(2,1)S(1)}, u32[]{:S(2)}, u32[]{:S(2)}) %all-to-all-start.1) | async-done | bytes 1048608 | tf_op jit(solution)/shard_map/while/body/eval_jaxpr/all_to_all | solution.py:40
  634.3 5.3 collective-permute-start
  640.7 10.1 %collective-permute-done = bf16[2048,128]{1,0:T(8,128)(2,1)S(1)} collective-permute-done((bf16[2048,128]{1,0:T(8,128)(2,1)S(1)}, bf16[2048,128]{1,0:T(8,128)(2,1)S(1)}, u32[]{:S(2)}, u32[]{:S(2)}) %collective-permute-start) | collective-permute-done | bytes 524320 | tf_op jit(solution)/shard_map/while/body/eval_jaxpr/ppermute | solution.py:10
  678.9 7.6 all-to-all-done
  698.2 13.5 %all-to-all-done.1 = bf16[32,128,128]{2,1,0:T(8,128)(2,1)S(1)} async-done(((bf16[32,128,128]{2,1,0:T(8,128)(2,1)}), bf16[32,128,128]{2,1,0:T(8,128)(2,1)S(1)}, u32[]{:S(2)}, u32[]{:S(2)}) %all-to-all-start.1) | async-done | bytes 1048608 | tf_op jit(solution)/shard_map/while/body/eval_jaxpr/all_to_all | solution.py:40
  714.7 5.3 collective-permute-start
  721.1 10.1 %collective-permute-done = bf16[2048,128]{1,0:T(8,128)(2,1)S(1)} collective-permute-done((bf16[2048,128]{1,0:T(8,128)(2,1)S(1)}, bf16[2048,128]{1,0:T(8,128)(2,1)S(1)}, u32[]{:S(2)}, u32[]{:S(2)}) %collective-permute-start) | collective-permute-done | bytes 524320 | tf_op jit(solution)/shard_map/while/body/eval_jaxpr/ppermute | solution.py:10
  759.2 7.6 all-to-all-done
  778.5 13.5 %all-to-all-done.1 = bf16[32,128,128]{2,1,0:T(8,128)(2,1)S(1)} async-done(((bf16[32,128,128]{2,1,0:T(8,128)(2,1)}), bf16[32,128,128]{2,1,0:T(8,128)(2,1)S(1)}, u32[]{:S(2)}, u32[]{:S(2)}) %all-to-all-start.1) | async-done | bytes 1048608 | tf_op jit(solution)/shard_map/while/body/eval_jaxpr/all_to_all | solution.py:40
  795.0 5.4 collective-permute-start
  801.5 10.1 %collective-permute-done = bf16[2048,128]{1,0:T(8,128)(2,1)S(1)} collective-permute-done((bf16[2048,128]{1,0:T(8,128)(2,1)S(1)}, bf16[2048,128]{1,0:T(8,128)(2,1)S(1)}, u32[]{:S(2)}, u32[]{:S(2)}) %collective-permute-start) | collective-permute-done | bytes 524320 | tf_op jit(solution)/shard_map/while/body/eval_jaxpr/ppermute | solution.py:10
  839.6 7.6 all-to-all-done
  858.9 13.5 %all-to-all-done.1 = bf16[32,128,128]{2,1,0:T(8,128)(2,1)S(1)} async-done(((bf16[32,128,128]{2,1,0:T(8,128)(2,1)}), bf16[32,128,128]{2,1,0:T(8,128)(2,1)S(1)}, u32[]{:S(2)}, u32[]{:S(2)}) %all-to-all-start.1) | async-done | bytes 1048608 | tf_op jit(solution)/shard_map/while/body/eval_jaxpr/all_to_all | solution.py:40
  875.4 5.3 collective-permute-start
  881.8 10.1 %collective-permute-done = bf16[2048,128]{1,0:T(8,128)(2,1)S(1)} collective-permute-done((bf16[2048,128]{1,0:T(8,128)(2,1)S(1)}, bf16[2048,128]{1,0:T(8,128)(2,1)S(1)}, u32[]{:S(2)}, u32[]{:S(2)}) %collective-permute-start) | collective-permute-done | bytes 524320 | tf_op jit(solution)/shard_map/while/body/eval_jaxpr/ppermute | solution.py:10
  891.9 43.8 %reduce-scatter.2.cloned.1.call-done = bf16[4,16,2048]{2,1,0:T(8,128)(2,1)} async-done(((bf16[4,128,2048]{2,1,0:T(8,128)(2,1)}), bf16[4,16,2048]{2,1,0:T(8,128)(2,1)}) %reduce-scatter.2.cloned.1.call-update) | async-done | bytes 262160 | tf_op jit(solution)/shard_map/reduce_scatter | solution.py:88
  (943 shorter events, 470.0 us)
Async XLA Ops:
  6.5 929.2 %reduce-scatter.2.cloned.1.call-start = ((), (), s32[]{:S(2)}) async-start(), calls=%async_computation.3 | async-start | bytes 2359296 | tf_op jit(solution)/shard_map/reduce_scatter | solution.py:88
  23.9 25.5 %all-to-all-start = ((bf16[32,128,128]{2,1,0:T(8,128)(2,1)}), bf16[32,128,128]{2,1,0:T(8,128)(2,1)S(1)}, u32[]{:S(2)}, u32[]{:S(2)}) async-start(bf16[32,128,128]{2,1,0:T(8,128)(2,1)} %bitcast.96), calls=%async_computation | async-start | bytes 2097152 | tf_op jit(solution)/shard_map/while/body/eval_jaxpr/all_to_all | solution.py:40
  53.9 20.9 %all-to-all-start.1 = ((bf16[32,128,128]{2,1,0:T(8,128)(2,1)}), bf16[32,128,128]{2,1,0:T(8,128)(2,1)S(1)}, u32[]{:S(2)}, u32[]{:S(2)}) async-start(bf16[32,128,128]{2,1,0:T(8,128)(2,1)} %bitcast.100), calls=%async_computation.1 | async-start | bytes 2097152 | tf_op jit(solution)/shard_map/while/body/eval_jaxpr/all_to_all | solution.py:40
  61.2 14.3 %copy-start.4 = (bf16[96,64,128]{2,1,0:T(8,128)(2,1)S(1)}, bf16[96,64,128]{2,1,0:T(8,128)(2,1)}, u32[]{:S(2)}) copy-start(bf16[96,64,128]{2,1,0:T(8,128)(2,1)} %broadcast_select_fusion.17) | copy-start | bytes 4718596 | tf_op jit(solution)/shard_map/while
  77.7 14.7 %collective-permute-start = (bf16[2048,128]{1,0:T(8,128)(2,1)S(1)}, bf16[2048,128]{1,0:T(8,128)(2,1)S(1)}, u32[]{:S(2)}, u32[]{:S(2)}) collective-permute-start(bf16[2048,128]{1,0:T(8,128)(2,1)S(1)} %get-tuple-element.859), channel_id=1, source_target_pairs={{0,32},{32,64},{64,96},{96,128},{128,160},{160,192},{192,224},{1,3... | collective-permute-start | bytes 1572872 | tf_op jit(solution)/shard_map/while/body/eval_jaxpr/ppermute | solution.py:10
  106.5 21.5 %all-to-all-start = ((bf16[32,128,128]{2,1,0:T(8,128)(2,1)}), bf16[32,128,128]{2,1,0:T(8,128)(2,1)S(1)}, u32[]{:S(2)}, u32[]{:S(2)}) async-start(bf16[32,128,128]{2,1,0:T(8,128)(2,1)} %bitcast.96), calls=%async_computation | async-start | bytes 2097152 | tf_op jit(solution)/shard_map/while/body/eval_jaxpr/all_to_all | solution.py:40
  132.5 20.8 %all-to-all-start.1 = ((bf16[32,128,128]{2,1,0:T(8,128)(2,1)}), bf16[32,128,128]{2,1,0:T(8,128)(2,1)S(1)}, u32[]{:S(2)}, u32[]{:S(2)}) async-start(bf16[32,128,128]{2,1,0:T(8,128)(2,1)} %bitcast.100), calls=%async_computation.1 | async-start | bytes 2097152 | tf_op jit(solution)/shard_map/while/body/eval_jaxpr/all_to_all | solution.py:40
  139.8 14.3 %copy-start.4 = (bf16[96,64,128]{2,1,0:T(8,128)(2,1)S(1)}, bf16[96,64,128]{2,1,0:T(8,128)(2,1)}, u32[]{:S(2)}) copy-start(bf16[96,64,128]{2,1,0:T(8,128)(2,1)} %broadcast_select_fusion.17) | copy-start | bytes 4718596 | tf_op jit(solution)/shard_map/while
  156.3 15.3 %collective-permute-start = (bf16[2048,128]{1,0:T(8,128)(2,1)S(1)}, bf16[2048,128]{1,0:T(8,128)(2,1)S(1)}, u32[]{:S(2)}, u32[]{:S(2)}) collective-permute-start(bf16[2048,128]{1,0:T(8,128)(2,1)S(1)} %get-tuple-element.859), channel_id=1, source_target_pairs={{0,32},{32,64},{64,96},{96,128},{128,160},{160,192},{192,224},{1,3... | collective-permute-start | bytes 1572872 | tf_op jit(solution)/shard_map/while/body/eval_jaxpr/ppermute | solution.py:10
  185.6 21.5 %all-to-all-start = ((bf16[32,128,128]{2,1,0:T(8,128)(2,1)}), bf16[32,128,128]{2,1,0:T(8,128)(2,1)S(1)}, u32[]{:S(2)}, u32[]{:S(2)}) async-start(bf16[32,128,128]{2,1,0:T(8,128)(2,1)} %bitcast.96), calls=%async_computation | async-start | bytes 2097152 | tf_op jit(solution)/shard_map/while/body/eval_jaxpr/all_to_all | solution.py:40
  199.6 8.3 copy-start.3
  211.6 20.9 %all-to-all-start.1 = ((bf16[32,128,128]{2,1,0:T(8,128)(2,1)}), bf16[32,128,128]{2,1,0:T(8,128)(2,1)S(1)}, u32[]{:S(2)}, u32[]{:S(2)}) async-start(bf16[32,128,128]{2,1,0:T(8,128)(2,1)} %bitcast.100), calls=%async_computation.1 | async-start | bytes 2097152 | tf_op jit(solution)/shard_map/while/body/eval_jaxpr/all_to_all | solution.py:40
  218.9 14.3 %copy-start.4 = (bf16[96,64,128]{2,1,0:T(8,128)(2,1)S(1)}, bf16[96,64,128]{2,1,0:T(8,128)(2,1)}, u32[]{:S(2)}) copy-start(bf16[96,64,128]{2,1,0:T(8,128)(2,1)} %broadcast_select_fusion.17) | copy-start | bytes 4718596 | tf_op jit(solution)/shard_map/while
  235.4 15.3 %collective-permute-start = (bf16[2048,128]{1,0:T(8,128)(2,1)S(1)}, bf16[2048,128]{1,0:T(8,128)(2,1)S(1)}, u32[]{:S(2)}, u32[]{:S(2)}) collective-permute-start(bf16[2048,128]{1,0:T(8,128)(2,1)S(1)} %get-tuple-element.859), channel_id=1, source_target_pairs={{0,32},{32,64},{64,96},{96,128},{128,160},{160,192},{192,224},{1,3... | collective-permute-start | bytes 1572872 | tf_op jit(solution)/shard_map/while/body/eval_jaxpr/ppermute | solution.py:10
  264.8 21.5 %all-to-all-start = ((bf16[32,128,128]{2,1,0:T(8,128)(2,1)}), bf16[32,128,128]{2,1,0:T(8,128)(2,1)S(1)}, u32[]{:S(2)}, u32[]{:S(2)}) async-start(bf16[32,128,128]{2,1,0:T(8,128)(2,1)} %bitcast.96), calls=%async_computation | async-start | bytes 2097152 | tf_op jit(solution)/shard_map/while/body/eval_jaxpr/all_to_all | solution.py:40
  278.8 8.3 copy-start.3
  290.8 20.9 %all-to-all-start.1 = ((bf16[32,128,128]{2,1,0:T(8,128)(2,1)}), bf16[32,128,128]{2,1,0:T(8,128)(2,1)S(1)}, u32[]{:S(2)}, u32[]{:S(2)}) async-start(bf16[32,128,128]{2,1,0:T(8,128)(2,1)} %bitcast.100), calls=%async_computation.1 | async-start | bytes 2097152 | tf_op jit(solution)/shard_map/while/body/eval_jaxpr/all_to_all | solution.py:40
  298.1 14.3 %copy-start.4 = (bf16[96,64,128]{2,1,0:T(8,128)(2,1)S(1)}, bf16[96,64,128]{2,1,0:T(8,128)(2,1)}, u32[]{:S(2)}) copy-start(bf16[96,64,128]{2,1,0:T(8,128)(2,1)} %broadcast_select_fusion.17) | copy-start | bytes 4718596 | tf_op jit(solution)/shard_map/while
  314.6 15.3 %collective-permute-start = (bf16[2048,128]{1,0:T(8,128)(2,1)S(1)}, bf16[2048,128]{1,0:T(8,128)(2,1)S(1)}, u32[]{:S(2)}, u32[]{:S(2)}) collective-permute-start(bf16[2048,128]{1,0:T(8,128)(2,1)S(1)} %get-tuple-element.859), channel_id=1, source_target_pairs={{0,32},{32,64},{64,96},{96,128},{128,160},{160,192},{192,224},{1,3... | collective-permute-start | bytes 1572872 | tf_op jit(solution)/shard_map/while/body/eval_jaxpr/ppermute | solution.py:10
  343.9 21.5 %all-to-all-start = ((bf16[32,128,128]{2,1,0:T(8,128)(2,1)}), bf16[32,128,128]{2,1,0:T(8,128)(2,1)S(1)}, u32[]{:S(2)}, u32[]{:S(2)}) async-start(bf16[32,128,128]{2,1,0:T(8,128)(2,1)} %bitcast.96), calls=%async_computation | async-start | bytes 2097152 | tf_op jit(solution)/shard_map/while/body/eval_jaxpr/all_to_all | solution.py:40
  357.9 8.3 copy-start.3
  369.9 20.8 %all-to-all-start.1 = ((bf16[32,128,128]{2,1,0:T(8,128)(2,1)}), bf16[32,128,128]{2,1,0:T(8,128)(2,1)S(1)}, u32[]{:S(2)}, u32[]{:S(2)}) async-start(bf16[32,128,128]{2,1,0:T(8,128)(2,1)} %bitcast.100), calls=%async_computation.1 | async-start | bytes 2097152 | tf_op jit(solution)/shard_map/while/body/eval_jaxpr/all_to_all | solution.py:40
  377.2 14.3 %copy-start.4 = (bf16[96,64,128]{2,1,0:T(8,128)(2,1)S(1)}, bf16[96,64,128]{2,1,0:T(8,128)(2,1)}, u32[]{:S(2)}) copy-start(bf16[96,64,128]{2,1,0:T(8,128)(2,1)} %broadcast_select_fusion.17) | copy-start | bytes 4718596 | tf_op jit(solution)/shard_map/while
  393.7 16.0 %collective-permute-start = (bf16[2048,128]{1,0:T(8,128)(2,1)S(1)}, bf16[2048,128]{1,0:T(8,128)(2,1)S(1)}, u32[]{:S(2)}, u32[]{:S(2)}) collective-permute-start(bf16[2048,128]{1,0:T(8,128)(2,1)S(1)} %get-tuple-element.859), channel_id=1, source_target_pairs={{0,32},{32,64},{64,96},{96,128},{128,160},{160,192},{192,224},{1,3... | collective-permute-start | bytes 1572872 | tf_op jit(solution)/shard_map/while/body/eval_jaxpr/ppermute | solution.py:10
  423.8 21.5 %all-to-all-start = ((bf16[32,128,128]{2,1,0:T(8,128)(2,1)}), bf16[32,128,128]{2,1,0:T(8,128)(2,1)S(1)}, u32[]{:S(2)}, u32[]{:S(2)}) async-start(bf16[32,128,128]{2,1,0:T(8,128)(2,1)} %bitcast.96), calls=%async_computation | async-start | bytes 2097152 | tf_op jit(solution)/shard_map/while/body/eval_jaxpr/all_to_all | solution.py:40
  449.8 20.8 %all-to-all-start.1 = ((bf16[32,128,128]{2,1,0:T(8,128)(2,1)}), bf16[32,128,128]{2,1,0:T(8,128)(2,1)S(1)}, u32[]{:S(2)}, u32[]{:S(2)}) async-start(bf16[32,128,128]{2,1,0:T(8,128)(2,1)} %bitcast.100), calls=%async_computation.1 | async-start | bytes 2097152 | tf_op jit(solution)/shard_map/while/body/eval_jaxpr/all_to_all | solution.py:40
  457.1 14.3 %copy-start.4 = (bf16[96,64,128]{2,1,0:T(8,128)(2,1)S(1)}, bf16[96,64,128]{2,1,0:T(8,128)(2,1)}, u32[]{:S(2)}) copy-start(bf16[96,64,128]{2,1,0:T(8,128)(2,1)} %broadcast_select_fusion.17) | copy-start | bytes 4718596 | tf_op jit(solution)/shard_map/while
  473.6 16.5 %collective-permute-start = (bf16[2048,128]{1,0:T(8,128)(2,1)S(1)}, bf16[2048,128]{1,0:T(8,128)(2,1)S(1)}, u32[]{:S(2)}, u32[]{:S(2)}) collective-permute-start(bf16[2048,128]{1,0:T(8,128)(2,1)S(1)} %get-tuple-element.859), channel_id=1, source_target_pairs={{0,32},{32,64},{64,96},{96,128},{128,160},{160,192},{192,224},{1,3... | collective-permute-start | bytes 1572872 | tf_op jit(solution)/shard_map/while/body/eval_jaxpr/ppermute | solution.py:10
  504.2 21.5 %all-to-all-start = ((bf16[32,128,128]{2,1,0:T(8,128)(2,1)}), bf16[32,128,128]{2,1,0:T(8,128)(2,1)S(1)}, u32[]{:S(2)}, u32[]{:S(2)}) async-start(bf16[32,128,128]{2,1,0:T(8,128)(2,1)} %bitcast.96), calls=%async_computation | async-start | bytes 2097152 | tf_op jit(solution)/shard_map/while/body/eval_jaxpr/all_to_all | solution.py:40
  530.2 20.8 %all-to-all-start.1 = ((bf16[32,128,128]{2,1,0:T(8,128)(2,1)}), bf16[32,128,128]{2,1,0:T(8,128)(2,1)S(1)}, u32[]{:S(2)}, u32[]{:S(2)}) async-start(bf16[32,128,128]{2,1,0:T(8,128)(2,1)} %bitcast.100), calls=%async_computation.1 | async-start | bytes 2097152 | tf_op jit(solution)/shard_map/while/body/eval_jaxpr/all_to_all | solution.py:40
  537.5 14.3 %copy-start.4 = (bf16[96,64,128]{2,1,0:T(8,128)(2,1)S(1)}, bf16[96,64,128]{2,1,0:T(8,128)(2,1)}, u32[]{:S(2)}) copy-start(bf16[96,64,128]{2,1,0:T(8,128)(2,1)} %broadcast_select_fusion.17) | copy-start | bytes 4718596 | tf_op jit(solution)/shard_map/while
  553.9 16.5 %collective-permute-start = (bf16[2048,128]{1,0:T(8,128)(2,1)S(1)}, bf16[2048,128]{1,0:T(8,128)(2,1)S(1)}, u32[]{:S(2)}, u32[]{:S(2)}) collective-permute-start(bf16[2048,128]{1,0:T(8,128)(2,1)S(1)} %get-tuple-element.859), channel_id=1, source_target_pairs={{0,32},{32,64},{64,96},{96,128},{128,160},{160,192},{192,224},{1,3... | collective-permute-start | bytes 1572872 | tf_op jit(solution)/shard_map/while/body/eval_jaxpr/ppermute | solution.py:10
  584.5 21.5 %all-to-all-start = ((bf16[32,128,128]{2,1,0:T(8,128)(2,1)}), bf16[32,128,128]{2,1,0:T(8,128)(2,1)S(1)}, u32[]{:S(2)}, u32[]{:S(2)}) async-start(bf16[32,128,128]{2,1,0:T(8,128)(2,1)} %bitcast.96), calls=%async_computation | async-start | bytes 2097152 | tf_op jit(solution)/shard_map/while/body/eval_jaxpr/all_to_all | solution.py:40
  610.5 20.8 %all-to-all-start.1 = ((bf16[32,128,128]{2,1,0:T(8,128)(2,1)}), bf16[32,128,128]{2,1,0:T(8,128)(2,1)S(1)}, u32[]{:S(2)}, u32[]{:S(2)}) async-start(bf16[32,128,128]{2,1,0:T(8,128)(2,1)} %bitcast.100), calls=%async_computation.1 | async-start | bytes 2097152 | tf_op jit(solution)/shard_map/while/body/eval_jaxpr/all_to_all | solution.py:40
  617.8 14.3 %copy-start.4 = (bf16[96,64,128]{2,1,0:T(8,128)(2,1)S(1)}, bf16[96,64,128]{2,1,0:T(8,128)(2,1)}, u32[]{:S(2)}) copy-start(bf16[96,64,128]{2,1,0:T(8,128)(2,1)} %broadcast_select_fusion.17) | copy-start | bytes 4718596 | tf_op jit(solution)/shard_map/while
  634.3 16.5 %collective-permute-start = (bf16[2048,128]{1,0:T(8,128)(2,1)S(1)}, bf16[2048,128]{1,0:T(8,128)(2,1)S(1)}, u32[]{:S(2)}, u32[]{:S(2)}) collective-permute-start(bf16[2048,128]{1,0:T(8,128)(2,1)S(1)} %get-tuple-element.859), channel_id=1, source_target_pairs={{0,32},{32,64},{64,96},{96,128},{128,160},{160,192},{192,224},{1,3... | collective-permute-start | bytes 1572872 | tf_op jit(solution)/shard_map/while/body/eval_jaxpr/ppermute | solution.py:10
  664.9 21.5 %all-to-all-start = ((bf16[32,128,128]{2,1,0:T(8,128)(2,1)}), bf16[32,128,128]{2,1,0:T(8,128)(2,1)S(1)}, u32[]{:S(2)}, u32[]{:S(2)}) async-start(bf16[32,128,128]{2,1,0:T(8,128)(2,1)} %bitcast.96), calls=%async_computation | async-start | bytes 2097152 | tf_op jit(solution)/shard_map/while/body/eval_jaxpr/all_to_all | solution.py:40
  690.9 20.8 %all-to-all-start.1 = ((bf16[32,128,128]{2,1,0:T(8,128)(2,1)}), bf16[32,128,128]{2,1,0:T(8,128)(2,1)S(1)}, u32[]{:S(2)}, u32[]{:S(2)}) async-start(bf16[32,128,128]{2,1,0:T(8,128)(2,1)} %bitcast.100), calls=%async_computation.1 | async-start | bytes 2097152 | tf_op jit(solution)/shard_map/while/body/eval_jaxpr/all_to_all | solution.py:40
  698.2 14.3 %copy-start.4 = (bf16[96,64,128]{2,1,0:T(8,128)(2,1)S(1)}, bf16[96,64,128]{2,1,0:T(8,128)(2,1)}, u32[]{:S(2)}) copy-start(bf16[96,64,128]{2,1,0:T(8,128)(2,1)} %broadcast_select_fusion.17) | copy-start | bytes 4718596 | tf_op jit(solution)/shard_map/while
  714.7 16.5 %collective-permute-start = (bf16[2048,128]{1,0:T(8,128)(2,1)S(1)}, bf16[2048,128]{1,0:T(8,128)(2,1)S(1)}, u32[]{:S(2)}, u32[]{:S(2)}) collective-permute-start(bf16[2048,128]{1,0:T(8,128)(2,1)S(1)} %get-tuple-element.859), channel_id=1, source_target_pairs={{0,32},{32,64},{64,96},{96,128},{128,160},{160,192},{192,224},{1,3... | collective-permute-start | bytes 1572872 | tf_op jit(solution)/shard_map/while/body/eval_jaxpr/ppermute | solution.py:10
  745.2 21.5 %all-to-all-start = ((bf16[32,128,128]{2,1,0:T(8,128)(2,1)}), bf16[32,128,128]{2,1,0:T(8,128)(2,1)S(1)}, u32[]{:S(2)}, u32[]{:S(2)}) async-start(bf16[32,128,128]{2,1,0:T(8,128)(2,1)} %bitcast.96), calls=%async_computation | async-start | bytes 2097152 | tf_op jit(solution)/shard_map/while/body/eval_jaxpr/all_to_all | solution.py:40
  771.2 20.8 %all-to-all-start.1 = ((bf16[32,128,128]{2,1,0:T(8,128)(2,1)}), bf16[32,128,128]{2,1,0:T(8,128)(2,1)S(1)}, u32[]{:S(2)}, u32[]{:S(2)}) async-start(bf16[32,128,128]{2,1,0:T(8,128)(2,1)} %bitcast.100), calls=%async_computation.1 | async-start | bytes 2097152 | tf_op jit(solution)/shard_map/while/body/eval_jaxpr/all_to_all | solution.py:40
  778.5 14.3 %copy-start.4 = (bf16[96,64,128]{2,1,0:T(8,128)(2,1)S(1)}, bf16[96,64,128]{2,1,0:T(8,128)(2,1)}, u32[]{:S(2)}) copy-start(bf16[96,64,128]{2,1,0:T(8,128)(2,1)} %broadcast_select_fusion.17) | copy-start | bytes 4718596 | tf_op jit(solution)/shard_map/while
  795.0 16.5 %collective-permute-start = (bf16[2048,128]{1,0:T(8,128)(2,1)S(1)}, bf16[2048,128]{1,0:T(8,128)(2,1)S(1)}, u32[]{:S(2)}, u32[]{:S(2)}) collective-permute-start(bf16[2048,128]{1,0:T(8,128)(2,1)S(1)} %get-tuple-element.859), channel_id=1, source_target_pairs={{0,32},{32,64},{64,96},{96,128},{128,160},{160,192},{192,224},{1,3... | collective-permute-start | bytes 1572872 | tf_op jit(solution)/shard_map/while/body/eval_jaxpr/ppermute | solution.py:10
  825.6 21.5 %all-to-all-start = ((bf16[32,128,128]{2,1,0:T(8,128)(2,1)}), bf16[32,128,128]{2,1,0:T(8,128)(2,1)S(1)}, u32[]{:S(2)}, u32[]{:S(2)}) async-start(bf16[32,128,128]{2,1,0:T(8,128)(2,1)} %bitcast.96), calls=%async_computation | async-start | bytes 2097152 | tf_op jit(solution)/shard_map/while/body/eval_jaxpr/all_to_all | solution.py:40
  851.6 20.8 %all-to-all-start.1 = ((bf16[32,128,128]{2,1,0:T(8,128)(2,1)}), bf16[32,128,128]{2,1,0:T(8,128)(2,1)S(1)}, u32[]{:S(2)}, u32[]{:S(2)}) async-start(bf16[32,128,128]{2,1,0:T(8,128)(2,1)} %bitcast.100), calls=%async_computation.1 | async-start | bytes 2097152 | tf_op jit(solution)/shard_map/while/body/eval_jaxpr/all_to_all | solution.py:40
  858.9 14.3 %copy-start.4 = (bf16[96,64,128]{2,1,0:T(8,128)(2,1)S(1)}, bf16[96,64,128]{2,1,0:T(8,128)(2,1)}, u32[]{:S(2)}) copy-start(bf16[96,64,128]{2,1,0:T(8,128)(2,1)} %broadcast_select_fusion.17) | copy-start | bytes 4718596 | tf_op jit(solution)/shard_map/while
  875.4 16.5 %collective-permute-start = (bf16[2048,128]{1,0:T(8,128)(2,1)S(1)}, bf16[2048,128]{1,0:T(8,128)(2,1)S(1)}, u32[]{:S(2)}, u32[]{:S(2)}) collective-permute-start(bf16[2048,128]{1,0:T(8,128)(2,1)S(1)} %get-tuple-element.859), channel_id=1, source_target_pairs={{0,32},{32,64},{64,96},{96,128},{128,160},{160,192},{192,224},{1,3... | collective-permute-start | bytes 1572872 | tf_op jit(solution)/shard_map/while/body/eval_jaxpr/ppermute | solution.py:10
  (43 other events, 174.3 us)
Sparse Core Ops, SparseCore 0:
  892.0 43.6 reduce-scatter.1
where the time goes:
time: 950 us; the launch traced here: 943 us
  waiting for transfers between devices  387 us (41%)
  local copies, waits for them, and re-layouts  245 us (26%)
  starting transfers between devices  150 us (16%)
  other arithmetic  105 us (11%)
  matrix products  38.3 us (4%)
  between operations  13.4 us (1%)
    all_to_all x22, waiting for transfers between devices, run_layer(): lax.all_to_all(outgoing, 'neuron', split_axis=0, concat_axis=0, tiled=True)  232 us
    ppermute x11, waiting for transfers between devices, from_behind(): lax.ppermute(value, axis, [(source, source + steps) for source in range(l...  111 us
    all_to_all x22, starting transfers between devices, run_layer(): lax.all_to_all(outgoing, 'neuron', split_axis=0, concat_axis=0, tiled=True)  97.1 us
    scatter x22, local copies, waits for them, and re-layouts, slot_tables(): jnp.zeros((owners_count * capacity,), jnp.int32).at[target]  94.6 us
    ppermute x11, starting transfers between devices, from_behind(): lax.ppermute(value, axis, [(source, source + steps) for source in range(l...  52.9 us
    select_n x44, local copies, waits for them, and re-layouts, one_step(): gathered = jnp.where(keep, updated, gathered)  46 us
    reduce_scatter x1, waiting for transfers between devices, local(): lax.psum_scatter(gathered, 'segment', scatter_dimension=1, tiled=True)  43.8 us
    dot_general x22, matrix products, run_layer(): jnp.einsum('bok,bkr->bor', shaped, joined, preferred_element_type=jnp.flo...  38.3 us
  transfers between devices with their start and end apart: 34, of which 34 were waited for; matrix products, arithmetic and copies ran while one was open for 15% of the time, Pallas kernels for 0%

commit v1 on v0

v1 whole, which is shorter than its diff:
```python
import functools

import jax
import jax.numpy as jnp
from jax import lax
from jax.experimental import pallas as pl
from jax.experimental.pallas import tpu as pltpu
from jax.sharding import PartitionSpec as P

MESH = pl.DeviceIdType.MESH
BLK = 64
CHUNKS = 8
SKEW = 2
GROUP = 8


def tables(cols, near, owners, me):
    layers = cols.shape[0]
    grid = cols.reshape(layers, owners, -1)
    per = grid.shape[2]
    place = lax.broadcasted_iota(jnp.int32, grid.shape, 2)
    asked = (grid // per) == me
    first = jnp.min(jnp.where(asked, place, per - 1), axis=2, keepdims=True)
    last = jnp.max(jnp.where(asked, place, 0), axis=2, keepdims=True)
    inside = grid % per
    send = jnp.concatenate(
        [
            jnp.sum(jnp.where(place == first, inside, 0), axis=2),
            jnp.sum(jnp.where(place == last, inside, 0), axis=2),
        ],
        axis=1,
    )
    mine = lax.dynamic_index_in_dim(grid, me, 1, keepdims=False) // per
    same = mine[:, :, None] == mine[:, None, :]
    earlier = lax.broadcasted_iota(jnp.int32, same.shape, 2) < lax.broadcasted_iota(
        jnp.int32, same.shape, 1
    )
    slot = jnp.max(jnp.where(same & earlier, 1, 0), axis=2)
    row = lambda v: jnp.pad(v, ((0, 0), (0, 128 - v.shape[1])))
    far = jnp.concatenate([mine, slot], axis=1)
    packed = jnp.stack(
        [row(send), row(near.reshape(layers, -1)), row(far), jnp.zeros((layers, 128), jnp.int32)],
        axis=1,
    )
    return packed.reshape(layers * 4, 128)


def kernel(
    dims, x_ref, w_ref, b_ref, t_ref, o_ref,
    act_even, act_odd, total, send, recv_even, recv_odd, wbuf, ball, btr, tall, tabs,
    local_sem, small_send, small_recv, a2a_send, a2a_recv, ring_send, ring_recv,
):
    sections, owners, per, layers, rows = dims
    own = layers // sections
    half = per // 2
    step = half // CHUNKS
    s = lax.axis_index("segment")
    me = lax.axis_index("neuron")
    ahead = lax.rem(s + 1, sections)
    behind = lax.rem(s + sections - 1, sections)
    last = sections - 1

    loads = [
        pltpu.make_async_copy(x_ref, act_even, local_sem.at[0]),
        pltpu.make_async_copy(w_ref, wbuf.at[pl.ds(s * own, own)], local_sem.at[1]),
    ]
    for load in loads:
        load.start()
    tall[pl.ds(s, 1)] = t_ref[...][None]
    ball[pl.ds(s * own, own)] = b_ref[...]

    barrier = pltpu.get_barrier_semaphore()

    def greet(d, carry):
        pl.semaphore_signal(
            barrier, inc=1, device_id={"neuron": lax.rem(me + d, owners)}, device_id_type=MESH
        )
        return carry

    lax.fori_loop(1, owners, greet, 0)

    def greet_section(d, carry):
        pl.semaphore_signal(
            barrier, inc=1, device_id={"segment": lax.rem(s + d, sections)}, device_id_type=MESH
        )
        return carry

    lax.fori_loop(1, sections, greet_section, 0)
    pl.semaphore_wait(barrier, owners - 1 + sections - 1)

    def share(d, carry):
        to = {"segment": lax.rem(s + d, sections)}
        pltpu.make_async_remote_copy(
            src_ref=tall.at[pl.ds(s, 1)], dst_ref=tall.at[pl.ds(s, 1)],
            send_sem=small_send.at[0], recv_sem=small_recv.at[0],
            device_id=to, device_id_type=MESH,
        ).start()
        pltpu.make_async_remote_copy(
            src_ref=ball.at[pl.ds(s * own, own)], dst_ref=ball.at[pl.ds(s * own, own)],
            send_sem=small_send.at[1], recv_sem=small_recv.at[1],
            device_id=to, device_id_type=MESH,
        ).start()
        return carry

    lax.fori_loop(1, sections, share, 0)

    def ring(source, layer, part, side, to):
        at = pl.ds(side * half + part * step, step)
        return pltpu.make_async_remote_copy(
            src_ref=source.at[at], dst_ref=wbuf.at[layer, at],
            send_sem=ring_send.at[side, layer], recv_sem=ring_recv.at[side, layer, part],
            device_id={"segment": to}, device_id_type=MESH,
        )

    def start_own(i, carry):
        t, part = i // CHUNKS, i % CHUNKS
        ring(w_ref.at[t], s * own + t, part, 0, ahead).start()
        ring(w_ref.at[t], s * own + t, part, 1, behind).start()
        return carry

    lax.fori_loop(0, own * CHUNKS, start_own, 0)

    parts = own * CHUNKS
    wide, tight = parts + SKEW, parts - SKEW

    def hand_on(k, side, to, fine, far_off):
        copy = ring(wbuf.at[k // CHUNKS], k // CHUNKS, lax.rem(k, CHUNKS), side, to)

        @pl.when(fine)
        def _():
            copy.wait_recv()

        @pl.when(fine & (far_off < last))
        def _():
            copy.start()

    def ring_step(e):
        t = e - SKEW * s
        early = t < tight * s + SKEW
        t = jnp.where(early, t, t - SKEW * sections)
        low, high = jnp.where(early, 0, s + 1), jnp.where(early, s, sections)
        h = jnp.maximum(t, 0) // tight
        rest = t - h * tight
        for home, fits in ((h - 1, rest < SKEW), (h, t >= 0)):
            fine = fits & (home >= low) & (home < high)
            k = jnp.clip(t + SKEW * home, 0, parts * sections - 1)
            hand_on(k, 0, ahead, fine, lax.rem(s - home + sections, sections))
        t = e + SKEW * s
        early = t < wide * s + tight
        t = jnp.where(early, t - SKEW * sections, t)
        low, high = jnp.where(early, 0, s + 1), jnp.where(early, s, sections)
        h = jnp.maximum(t, 0) // wide
        fine = (t >= 0) & (t - h * wide < parts) & (h >= low) & (h < high)
        k = jnp.clip(t - SKEW * h, 0, parts * sections - 1)
        hand_on(k, 1, behind, fine, lax.rem(h - s + sections, sections))

    def ring_steps(low, count):
        def one(i, carry):
            ring_step(low + i)
            return carry

        lax.fori_loop(0, count, one, 0)

    pltpu.make_async_copy(
        tall.at[pl.ds(0, sections - 1)], tall.at[pl.ds(0, sections - 1)], small_recv.at[0]
    ).wait()
    table_load = pltpu.make_async_copy(tall, tabs, local_sem.at[2])
    table_load.start()
    pltpu.make_async_copy(
        ball.at[pl.ds(0, layers - own)], ball.at[pl.ds(0, layers - own)], small_recv.at[1]
    ).wait()
    for i in range(per // 2):
        rows_of = jnp.concatenate(
            [
                jnp.zeros((BLK, 128), jnp.float32),
                ball[:, i, :],
                jnp.zeros((BLK - layers, 128), jnp.float32),
            ],
            axis=0,
        )
        btr[2 * i : 2 * i + 2] = rows_of.T.astype(jnp.bfloat16).reshape(2, BLK, 128)
    table_load.wait()
    for load in loads:
        load.wait()

    low_lanes = lax.broadcasted_iota(jnp.int32, (BLK, 128), 1) < BLK
    lead = SKEW * last + CHUNKS

    def one_layer(layer, now):
        act, after = (act_even, act_odd)[now], (act_odd, act_even)[now]
        recv = (recv_even, recv_odd)[now]
        home, base = layer // own, lax.rem(layer, own) * 4
        step_at = lead + layer * CHUNKS

        @pl.when(layer >= 2)
        def _():
            sent = send.at[now, pl.ds(0, owners - 1)]
            pltpu.make_async_copy(sent, sent, a2a_send.at[now]).wait()

        def pair(q):
            first = tabs[home, base, q]
            second = tabs[home, base, owners + q]
            return jnp.where(low_lanes, act[first], act[second])

        def give(d, c):
            q = lax.rem(me + d, owners)
            send[now, q] = pair(q)
            pltpu.make_async_remote_copy(
                src_ref=send.at[now, q], dst_ref=recv.at[me],
                send_sem=a2a_send.at[now], recv_sem=a2a_recv.at[now],
                device_id={"neuron": q}, device_id_type=MESH,
            ).start()
            return c

        lax.fori_loop(1, owners, give, 0)
        recv[me] = pair(me)

        @pl.when(layer == 0)
        def _():
            ring_steps(0, lead)

        ring_steps(step_at, CHUNKS // 4)
        pick = jnp.where(
            lax.broadcasted_iota(jnp.int32, (BLK, 128), 0) == layer, 1.0, 0.0
        ).astype(jnp.bfloat16)

        def near_group(g, c):
            joined, packed = [], []
            for i in range(GROUP):
                j = g * GROUP + i
                near = [act[tabs[home, base + 1, 3 * j + k]] for k in range(3)]
                joined.append(jnp.concatenate(near + [pick], axis=0))
                w = wbuf[layer, j]
                packed.append(
                    jnp.concatenate(
                        [w[:, :128], jnp.where(low_lanes, w[:, 128:], btr[j])], axis=1
                    )
                )
            sums = [
                jnp.dot(p, x, preferred_element_type=jnp.float32) for p, x in zip(packed, joined)
            ]
            for i in range(GROUP):
                total[g * GROUP + i] = sums[i]
            return c

        groups = per // GROUP

        def near_and_feed(g, c):
            near_group(g, c)
            ring_step(step_at + CHUNKS // 4 + g)
            return c

        fed = min(groups, CHUNKS // 2)
        lax.fori_loop(0, fed, near_and_feed, 0)
        lax.fori_loop(fed, groups, near_group, 0)
        got = recv.at[pl.ds(0, owners - 1)]
        pltpu.make_async_copy(got, got, a2a_recv.at[now]).wait()

        def far_group(g, c):
            pairs, straights, sums, done = [], [], [], []
            for i in range(GROUP):
                j = g * GROUP + i
                pairs.append(recv[tabs[home, base + 2, j]])
                slot = jnp.zeros((BLK, 128), jnp.int32) + tabs[home, base + 2, per + j]
                straights.append(low_lanes == (slot == 0))
            for i in range(GROUP):
                joined = jnp.concatenate([jnp.zeros((BLK, 128), jnp.bfloat16), pairs[i]], axis=0)
                w = wbuf[layer, g * GROUP + i][:, 128:]
                sums.append(jnp.dot(w, joined, preferred_element_type=jnp.float32))
            for i in range(GROUP):
                far = jnp.where(straights[i], sums[i], pltpu.roll(sums[i], BLK, 1))
                z = total[g * GROUP + i] + far
                done.append(jnp.minimum(jnp.maximum(z, 0.0), 32.0).astype(jnp.bfloat16))
            for i in range(GROUP):
                after[g * GROUP + i] = done[i]
            return c

        lax.fori_loop(0, groups // 2, far_group, 0)
        ring_step(step_at + CHUNKS - CHUNKS // 4)
        lax.fori_loop(groups // 2, groups, far_group, 0)
        ring_steps(step_at + CHUNKS - CHUNKS // 4 + 1, CHUNKS // 4 - 1)

    def two_layers(i, carry):
        one_layer(2 * i, 0)
        one_layer(2 * i + 1, 1)
        return carry

    lax.fori_loop(0, layers // 2, two_layers, 0)
    o_ref[...] = act_even[...]

    for par in range(2):
        sent = send.at[par, pl.ds(0, owners - 1)]
        pltpu.make_async_copy(sent, sent, a2a_send.at[par]).wait()

    def drain(layer, carry):
        home = layer // own
        for side, gone in (
            (0, lax.rem(s - home + sections, sections)),
            (1, lax.rem(home - s + sections, sections)),
        ):

            @pl.when(gone < last)
            def _():
                sent = wbuf.at[layer, pl.ds(side * half, half)]
                pltpu.make_async_copy(sent, sent, ring_send.at[side, layer]).wait()

        return carry

    lax.fori_loop(0, layers, drain, 0)
    out = tall.at[pl.ds(0, sections - 1)]
    pltpu.make_async_copy(out, out, small_send.at[0]).wait()
    out = ball.at[pl.ds(0, layers - own)]
    pltpu.make_async_copy(out, out, small_send.at[1]).wait()


def local(samples, weights, biases, near_blocks, remote_cols):
    batches, rows, width = samples.shape
    sections = lax.axis_size("segment")
    owners = lax.axis_size("neuron")
    s = lax.axis_index("segment")
    me = lax.axis_index("neuron")
    per = width // BLK
    own = weights.shape[0]
    layers = own * sections
    share = rows // sections
    count = batches * share
    mine = lax.dynamic_slice_in_dim(samples, s * share, share, 1).reshape(count, width)
    x = mine.T
    x = jnp.concatenate([x, x], axis=1).reshape(per, BLK, 128)
    table = tables(remote_cols, near_blocks, owners, me)
    bias = biases.astype(jnp.float32).reshape(own, width // 128, 128)
    dims = (sections, owners, per, layers, count)
    bf16, f32 = jnp.bfloat16, jnp.float32
    out = pl.pallas_call(
        functools.partial(kernel, dims),
        out_shape=jax.ShapeDtypeStruct((per, BLK, 128), bf16),
        in_specs=[
            pl.BlockSpec(memory_space=pl.ANY),
            pl.BlockSpec(memory_space=pl.ANY),
            pl.BlockSpec(memory_space=pltpu.VMEM),
            pl.BlockSpec(memory_space=pltpu.VMEM),
        ],
        out_specs=pl.BlockSpec(memory_space=pltpu.VMEM),
        scratch_shapes=[
            pltpu.VMEM((per, BLK, 128), bf16),
            pltpu.VMEM((per, BLK, 128), bf16),
            pltpu.VMEM((per, BLK, 128), f32),
            pltpu.VMEM((2, owners, BLK, 128), bf16),
            pltpu.VMEM((owners, BLK, 128), bf16),
            pltpu.VMEM((owners, BLK, 128), bf16),
            pltpu.VMEM((layers, per, BLK, 256), bf16),
            pltpu.VMEM((layers, width // 128, 128), f32),
            pltpu.VMEM((per, BLK, 128), bf16),
            pltpu.VMEM((sections, own * 4, 128), jnp.int32),
            pltpu.SMEM((sections, own * 4, 128), jnp.int32),
            pltpu.SemaphoreType.DMA((3,)),
            pltpu.SemaphoreType.DMA((2,)),
            pltpu.SemaphoreType.DMA((2,)),
            pltpu.SemaphoreType.DMA((2,)),
            pltpu.SemaphoreType.DMA((2,)),
            pltpu.SemaphoreType.DMA((2, layers)),
            pltpu.SemaphoreType.DMA((2, layers, CHUNKS)),
        ],
        compiler_params=pltpu.CompilerParams(
            collective_id=0, has_side_effects=True, vmem_limit_bytes=48 * 1024 * 1024
        ),
    )(x, weights.reshape(own, per, BLK, 256), bias, table)
    y = out.reshape(width, 128)[:, :count].T
    return y.reshape(batches, share, width)


def solution(mesh):
    return jax.shard_map(
        local,
        mesh=mesh,
        in_specs=(
            P(None, None, "neuron"),
            P("segment", "neuron", None),
            P("segment", "neuron"),
            P("segment", "neuron", None),
            P("segment", None),
        ),
        out_specs=P(None, "segment", "neuron"),
        check_vma=False,
    )
```

time: 950 us -> 321 us (0.34)
  waiting for transfers between devices: 387 us -> 0 us
  Pallas kernels: 0 us -> 314 us
  local copies, waits for them, and re-layouts: 245 us -> 4.59 us
  starting transfers between devices: 150 us -> 0 us
  other arithmetic: 105 us -> 1.7 us
  matrix products: 38.3 us -> 0 us
  between operations: 13.4 us -> 0.08 us
    pallas_call x0 -> x1, Pallas kernels: none -> 314 us  [local(): pl.pallas_call(functools.partial(kernel, dims), out_shape=jax.ShapeDtypeS...]
    all_to_all x22 -> x0, waiting for transfers between devices: 232 us -> none  [run_layer(): lax.all_to_all(outgoing, 'neuron', split_axis=0, concat_axis=0, tiled=True)]
    ppermute x11 -> x0, waiting for transfers between devices: 111 us -> none  [from_behind(): lax.ppermute(value, axis, [(source, source + steps) for source in range(l...]
    all_to_all x22 -> x0, starting transfers between devices: 97.1 us -> none  [run_layer(): lax.all_to_all(outgoing, 'neuron', split_axis=0, concat_axis=0, tiled=True)]
    scatter x22 -> x0, local copies, waits for them, and re-layouts: 94.6 us -> none  [slot_tables(): jnp.zeros((owners_count * capacity,), jnp.int32).at[target]]
    select_n x165 -> x1, other arithmetic: 64.3 us -> 0.01 us  [tables(): mine = lax.dynamic_index_in_dim(grid, me, 1, keepdims=False) // per]
    ppermute x11 -> x0, starting transfers between devices: 52.9 us -> none  [from_behind(): lax.ppermute(value, axis, [(source, source + steps) for source in range(l...]
    gather x66 -> x0, local copies, waits for them, and re-layouts: 49.4 us -> none  [the longest x22 18.7 us: run_layer(): jnp.take(blocks, near.reshape(-1), axis=0)]
  transfers between devices with their start and end apart: 34 -> 0, of which waited for: 34 -> 0; matrix products, arithmetic and copies ran while one was open for 15% -> 0% of each run, Pallas kernels for 0% -> 0%
where the time goes in v1:
time: 321 us
  Pallas kernels  314 us (98%)
  local copies, waits for them, and re-layouts  4.59 us (1%)
    pallas_call x1, Pallas kernels, local(): pl.pallas_call(functools.partial(kernel, dims), out_shape=jax.ShapeDtypeS...  314 us

profile of v1, /device:TPU:1, one launch (start us, length us, event | category | flops | bytes accessed | tf_op | source)
XLA Modules:
  0.0 320.8 jit_solution(13836423809403772846)
XLA Ops:
  0.0 0.0 copy-start
  0.0 0.1 pad.17.clone
  0.1 0.8 convert_bitcast_fusion
  0.9 0.8 reshape.64
  1.7 0.2 select_reduce_fusion
  1.9 0.1 pad_add_fusion.1
  2.0 0.2 select_reduce_fusion.4
  2.2 0.2 select_reduce_fusion.3
  2.4 0.1 pad_add_fusion
  2.5 0.8 copy.11
  3.3 0.1 reshape.65
  3.4 0.1 add_add_fusion
  3.5 0.0 copy-done
  3.5 0.3 copy.10
  3.8 0.0 copy-start.1
  3.8 1.6 copy-done.1
  5.4 314.4 %shard_map.55 = bf16[32,64,128]{2,1,0:T(8,128)(2,1)S(1)} custom-call(bf16[32,64,128]{2,1,0:T(8,128)(2,1)S(1)} %bitcast.28, bf16[2,32,64,256]{3,2,1,0:T(8,128)(2,1)S(1)} %bitcast.27, f32[2,16,128]{2,1,0:T(8,128)S(1)} %bitcast.30, s32[8,128]{1,0:T(8,128)S(1)} %bitcast.31), custom_call_target="tpu_custom_call" | custom-call | tf_op jit(solution)/shard_map/pallas_call | solution.py:334
  319.9 0.9 copy.14
  (10 shorter events, 0.1 us)
Async XLA Ops:
  0.0 3.5 %copy-start = (bf16[4,128,2048]{2,1,0:T(8,128)(2,1)S(1)}, bf16[4,128,2048]{2,1,0:T(8,128)(2,1)}, u32[]{:S(2)}) copy-start(bf16[4,128,2048]{2,1,0:T(8,128)(2,1)} %param.5) | copy-start | bytes 6291460
  3.8 1.6 copy-start.1

commit v2 on v1

--- a/solution.py
+++ b/solution.py
@@ -9,8 +9,12 @@
 
 MESH = pl.DeviceIdType.MESH
 BLK = 64
-CHUNKS = 8
-SKEW = 2
+UNIT = 2
+FIRST_SHARE = 8
+SECOND_SHARE = 7
+SKEW = 3
+LEAD = 31
+BEHIND = 5
 GROUP = 8
 
 
@@ -52,8 +56,6 @@
 ):
     sections, owners, per, layers, rows = dims
     own = layers // sections
-    half = per // 2
-    step = half // CHUNKS
     s = lax.axis_index("segment")
     me = lax.axis_index("neuron")
     ahead = lax.rem(s + 1, sections)
@@ -104,63 +106,105 @@
 
     lax.fori_loop(1, sections, share, 0)
 
-    def ring(source, layer, part, side, to):
-        at = pl.ds(side * half + part * step, step)
+    units = per // UNIT
+    first = (FIRST_SHARE, units - FIRST_SHARE)
+    second = (SECOND_SHARE, units - SECOND_SHARE)
+    window = (first[0] + second[0], first[1] + second[1])
+    lone = window[0] - SKEW
+    end = window[1] * sections
+
+    def ring(source, home, i, side, to, own_source):
+        later = (i >= first[side]).astype(jnp.int32)
+        begin = 0 if side == 0 else first[0] + later * (second[0] - first[0])
+        place = begin + i - later * first[side]
+        at = pl.ds(place * UNIT, UNIT)
+        layer = home * own + later
         return pltpu.make_async_remote_copy(
-            src_ref=source.at[at], dst_ref=wbuf.at[layer, at],
-            send_sem=ring_send.at[side, layer], recv_sem=ring_recv.at[side, layer, part],
+            src_ref=source.at[later if own_source else layer, at], dst_ref=wbuf.at[layer, at],
+            send_sem=ring_send.at[side, later], recv_sem=ring_recv.at[side, home, i],
             device_id={"segment": to}, device_id_type=MESH,
         )
 
-    def start_own(i, carry):
-        t, part = i // CHUNKS, i % CHUNKS
-        ring(w_ref.at[t], s * own + t, part, 0, ahead).start()
-        ring(w_ref.at[t], s * own + t, part, 1, behind).start()
-        return carry
-
-    lax.fori_loop(0, own * CHUNKS, start_own, 0)
-
-    parts = own * CHUNKS
-    wide, tight = parts + SKEW, parts - SKEW
-
-    def hand_on(k, side, to, fine, far_off):
-        copy = ring(wbuf.at[k // CHUNKS], k // CHUNKS, lax.rem(k, CHUNKS), side, to)
+    def hand_on(side, home, i, fine, hops):
+        home, i = jnp.clip(home, 0, last), jnp.clip(i, 0, window[side] - 1)
+        copy = ring(wbuf, home, i, side, (ahead, behind)[side], False)
 
         @pl.when(fine)
         def _():
             copy.wait_recv()
 
-        @pl.when(fine & (far_off < last))
+        @pl.when(fine & (hops < last))
         def _():
             copy.start()
 
+    own_base = jnp.where(s == last, SKEW * (last - 1), window[0] * s)
+    own_early = jnp.where(s == 0, window[1], jnp.minimum(window[1], SKEW * (sections - s)))
+    own_late = window[1] * (s - 1) + SKEW * (sections - s) - own_early
+
+    def give_own(side, i, fine):
+        @pl.when(fine)
+        def _():
+            i_in = jnp.clip(i, 0, window[side] - 1)
+            ring(w_ref, s, i_in, side, (ahead, behind)[side], True).start()
+
     def ring_step(e):
+        t = e - own_base
+        give_own(0, jnp.where(e < SKEW, e, t), (e < SKEW) | ((t >= SKEW) & (t < window[0])))
+        t = e - own_late
+        give_own(
+            1,
+            jnp.where(e < own_early, e, t),
+            (e < own_early) | ((s > 0) & (t >= own_early) & (t < window[1])),
+        )
+
+        inner = (e >= SKEW) & (e < SKEW * s)
+        home = jnp.where(inner, s - e // SKEW, -1)
+        i = lax.rem(e, SKEW)
         t = e - SKEW * s
-        early = t < tight * s + SKEW
-        t = jnp.where(early, t, t - SKEW * sections)
-        low, high = jnp.where(early, 0, s + 1), jnp.where(early, s, sections)
-        h = jnp.maximum(t, 0) // tight
-        rest = t - h * tight
-        for home, fits in ((h - 1, rest < SKEW), (h, t >= 0)):
-            fine = fits & (home >= low) & (home < high)
-            k = jnp.clip(t + SKEW * home, 0, parts * sections - 1)
-            hand_on(k, 0, ahead, fine, lax.rem(s - home + sections, sections))
-        t = e + SKEW * s
-        early = t < wide * s + tight
-        t = jnp.where(early, t - SKEW * sections, t)
-        low, high = jnp.where(early, 0, s + 1), jnp.where(early, s, sections)
-        h = jnp.maximum(t, 0) // wide
-        fine = (t >= 0) & (t - h * wide < parts) & (h >= low) & (h < high)
-        k = jnp.clip(t - SKEW * h, 0, parts * sections - 1)
-        hand_on(k, 1, behind, fine, lax.rem(h - s + sections, sections))
-
-    def ring_steps(low, count):
-        def one(i, carry):
-            ring_step(low + i)
+        fits = (s >= 1) & (t >= 0) & (t < window[0])
+        home, i = jnp.where(fits, 0, home), jnp.where(fits, t, i)
+        t = t - window[0]
+        fits = (t >= 0) & (t < lone * (s - 1))
+        t = jnp.maximum(t, 0)
+        home = jnp.where(fits, 1 + t // lone, home)
+        i = jnp.where(fits, SKEW + lax.rem(t, lone), i)
+        t = e - window[0] * (s + 1)
+        fits = (t >= 0) & (t < SKEW * (last - 1 - s))
+        t_in = jnp.maximum(t, 0)
+        home = jnp.where(fits, last - 1 - t_in // SKEW, home)
+        i = jnp.where(fits, lax.rem(t_in, SKEW), i)
+        t = t - SKEW * (last - 1 - s)
+        fits = (s < last) & (t >= 0) & (t < window[0])
+        home, i = jnp.where(fits, last, home), jnp.where(fits, t, i)
+        hand_on(0, home, i, home >= 0, lax.rem(s - home + sections, sections))
+
+        t = e - SKEW * (sections + 1 + s)
+        t_in = jnp.maximum(t, 0)
+        home = t_in // lone
+        fine = (t >= 0) & (home > s) & (home < last)
+        hand_on(0, home, SKEW + lax.rem(t_in, lone), fine, s - home + sections)
+
+        for t, low, high, hops in (
+            (e - SKEW * (sections - s), 0, s, sections - s),
+            (e + SKEW * s, s + 1, sections, -s),
+        ):
+            t_in = jnp.maximum(t, 0)
+            home = t_in // window[1]
+            fine = (t >= 0) & (home >= low) & (home < high)
+            hand_on(1, home, lax.rem(t_in, window[1]), fine, home + hops)
+
+    def ring_until(low, high):
+        def one(e, carry):
+            ring_step(e)
             return carry
 
-        lax.fori_loop(0, count, one, 0)
-
+        lax.fori_loop(low, high, one, 0)
+        return jnp.maximum(low, high)
+
+    def needed(layer):
+        return jnp.minimum(LEAD + layer * (end + BEHIND - LEAD) // (layers - 1), end)
+
+    done = ring_until(0, SKEW)
     pltpu.make_async_copy(
         tall.at[pl.ds(0, sections - 1)], tall.at[pl.ds(0, sections - 1)], small_recv.at[0]
     ).wait()
@@ -179,18 +223,24 @@
             axis=0,
         )
         btr[2 * i : 2 * i + 2] = rows_of.T.astype(jnp.bfloat16).reshape(2, BLK, 128)
+    done = ring_until(done, 2 * SKEW)
     table_load.wait()
     for load in loads:
         load.wait()
 
     low_lanes = lax.broadcasted_iota(jnp.int32, (BLK, 128), 1) < BLK
-    lead = SKEW * last + CHUNKS
-
-    def one_layer(layer, now):
+    batch = owners // 4
+
+    def one_layer(layer, now, done):
         act, after = (act_even, act_odd)[now], (act_odd, act_even)[now]
         recv = (recv_even, recv_odd)[now]
         home, base = layer // own, lax.rem(layer, own) * 4
-        step_at = lead + layer * CHUNKS
+        begin = jnp.maximum(done, needed(layer))
+        steps = jnp.maximum(needed(jnp.minimum(layer + 1, layers - 1)) - begin, 0)
+
+        def feed(done, portion):
+            return ring_until(done, begin + steps * portion // 8)
+
 
         @pl.when(layer >= 2)
         def _():
@@ -207,19 +257,19 @@
             send[now, q] = pair(q)
             pltpu.make_async_remote_copy(
                 src_ref=send.at[now, q], dst_ref=recv.at[me],
-                send_sem=a2a_send.at[now], recv_sem=a2a_recv.at[now],
+                send_sem=a2a_send.at[now], recv_sem=a2a_recv.at[now, d // batch],
                 device_id={"neuron": q}, device_id_type=MESH,
             ).start()
             return c
 
-        lax.fori_loop(1, owners, give, 0)
+        lax.fori_loop(1, owners // 2, give, 0)
+
+        done = ring_until(done, jnp.where(layer > 0, begin + steps // 8, 0))
+        lax.fori_loop(owners // 2, owners, give, 0)
         recv[me] = pair(me)
 
-        @pl.when(layer == 0)
-        def _():
-            ring_steps(0, lead)
-
-        ring_steps(step_at, CHUNKS // 4)
+        done = ring_until(done, needed(layer))
+        done = feed(done, 2)
         pick = jnp.where(
             lax.broadcasted_iota(jnp.int32, (BLK, 128), 0) == layer, 1.0, 0.0
         ).astype(jnp.bfloat16)
@@ -245,16 +295,13 @@
 
         groups = per // GROUP
 
-        def near_and_feed(g, c):
-            near_group(g, c)
-            ring_step(step_at + CHUNKS // 4 + g)
-            return c
-
-        fed = min(groups, CHUNKS // 2)
-        lax.fori_loop(0, fed, near_and_feed, 0)
-        lax.fori_loop(fed, groups, near_group, 0)
-        got = recv.at[pl.ds(0, owners - 1)]
-        pltpu.make_async_copy(got, got, a2a_recv.at[now]).wait()
+        lax.fori_loop(0, groups // 2, near_group, 0)
+        done = feed(done, 3)
+        lax.fori_loop(groups // 2, groups, near_group, 0)
+        for i in range(4):
+            done = feed(done, 4 + i)
+            got = recv.at[pl.ds(0, batch - 1 if i == 0 else batch)]
+            pltpu.make_async_copy(got, got, a2a_recv.at[now, i]).wait()
 
         def far_group(g, c):
             pairs, straights, sums, done = [], [], [], []
@@ -276,37 +323,27 @@
             return c
 
         lax.fori_loop(0, groups // 2, far_group, 0)
-        ring_step(step_at + CHUNKS - CHUNKS // 4)
+        done = feed(done, 8)
         lax.fori_loop(groups // 2, groups, far_group, 0)
-        ring_steps(step_at + CHUNKS - CHUNKS // 4 + 1, CHUNKS // 4 - 1)
-
-    def two_layers(i, carry):
-        one_layer(2 * i, 0)
-        one_layer(2 * i + 1, 1)
-        return carry
-
-    lax.fori_loop(0, layers // 2, two_layers, 0)
+        return done
+
+    def two_layers(i, done):
+        done = one_layer(2 * i, 0, done)
+        return one_layer(2 * i + 1, 1, done)
+
+    done = lax.fori_loop(0, layers // 2, two_layers, done)
+    ring_until(done, end)
     o_ref[...] = act_even[...]
 
     for par in range(2):
         sent = send.at[par, pl.ds(0, owners - 1)]
         pltpu.make_async_copy(sent, sent, a2a_send.at[par]).wait()
 
-    def drain(layer, carry):
-        home = layer // own
-        for side, gone in (
-            (0, lax.rem(s - home + sections, sections)),
-            (1, lax.rem(home - s + sections, sections)),
-        ):
-
-            @pl.when(gone < last)
-            def _():
-                sent = wbuf.at[layer, pl.ds(side * half, half)]
-                pltpu.make_async_copy(sent, sent, ring_send.at[side, layer]).wait()
-
-        return carry
-
-    lax.fori_loop(0, layers, drain, 0)
+    for side in (0, 1):
+        for t in range(own):
+            count = (first, second)[t][side] * UNIT
+            sent = wbuf.at[pl.ds(0, last), pl.ds(0, count)]
+            pltpu.make_async_copy(sent, sent, ring_send.at[side, t]).wait()
     out = tall.at[pl.ds(0, sections - 1)]
     pltpu.make_async_copy(out, out, small_send.at[0]).wait()
     out = ball.at[pl.ds(0, layers - own)]
@@ -357,9 +394,9 @@
             pltpu.SemaphoreType.DMA((2,)),
             pltpu.SemaphoreType.DMA((2,)),
             pltpu.SemaphoreType.DMA((2,)),
-            pltpu.SemaphoreType.DMA((2,)),
-            pltpu.SemaphoreType.DMA((2, layers)),
-            pltpu.SemaphoreType.DMA((2, layers, CHUNKS)),
+            pltpu.SemaphoreType.DMA((2, 4)),
+            pltpu.SemaphoreType.DMA((2, own)),
+            pltpu.SemaphoreType.DMA((2, sections, own * per // UNIT)),
         ],
         compiler_params=pltpu.CompilerParams(
             collective_id=0, has_side_effects=True, vmem_limit_bytes=48 * 1024 * 1024

time: 321 us -> 246 us (0.77)
  Pallas kernels: 314 us -> 239 us
    pallas_call x1, Pallas kernels: 314 us -> 239 us  [local(): pl.pallas_call(functools.partial(kernel, dims), out_shape=jax.ShapeDtypeS...]
where the time goes in v2:
time: 246 us
  Pallas kernels  239 us (97%)
  local copies, waits for them, and re-layouts  4.59 us (2%)
    pallas_call x1, Pallas kernels, local(): pl.pallas_call(functools.partial(kernel, dims), out_shape=jax.ShapeDtypeS...  239 us

profile of v2, /device:TPU:1, one launch (start us, length us, event | category | flops | bytes accessed | tf_op | source)
XLA Modules:
  0.0 245.7 jit_solution(8821254035901097064)
XLA Ops:
  0.0 0.0 copy-start
  0.0 0.1 pad.17.clone
  0.1 0.8 convert_bitcast_fusion
  0.9 0.8 reshape.64
  1.7 0.2 select_reduce_fusion
  1.9 0.1 pad_add_fusion.1
  2.0 0.2 select_reduce_fusion.4
  2.2 0.2 select_reduce_fusion.3
  2.4 0.1 pad_add_fusion
  2.5 0.8 copy.11
  3.3 0.1 reshape.65
  3.4 0.1 add_add_fusion
  3.5 0.0 copy-done
  3.5 0.3 copy.10
  3.8 0.0 copy-start.1
  3.8 1.6 copy-done.1
  5.4 239.3 %shard_map.55 = bf16[32,64,128]{2,1,0:T(8,128)(2,1)S(1)} custom-call(bf16[32,64,128]{2,1,0:T(8,128)(2,1)S(1)} %bitcast.28, bf16[2,32,64,256]{3,2,1,0:T(8,128)(2,1)S(1)} %bitcast.27, f32[2,16,128]{2,1,0:T(8,128)S(1)} %bitcast.30, s32[8,128]{1,0:T(8,128)S(1)} %bitcast.31), custom_call_target="tpu_custom_call" | custom-call | tf_op jit(solution)/shard_map/pallas_call | solution.py:371
  244.8 0.9 copy.14
  (10 shorter events, 0.1 us)
Async XLA Ops:
  0.0 3.5 %copy-start = (bf16[4,128,2048]{2,1,0:T(8,128)(2,1)S(1)}, bf16[4,128,2048]{2,1,0:T(8,128)(2,1)}, u32[]{:S(2)}) copy-start(bf16[4,128,2048]{2,1,0:T(8,128)(2,1)} %param.5) | copy-start | bytes 6291460
  3.8 1.6 copy-start.1

commit v3 on v2

--- a/solution.py
+++ b/solution.py
@@ -1,4 +1,5 @@
 import functools
+import math
 
 import jax
 import jax.numpy as jnp
@@ -15,7 +16,7 @@
 SKEW = 3
 LEAD = 31
 BEHIND = 5
-GROUP = 8
+GROUP = 16
 
 
 def tables(cols, near, owners, me):
@@ -230,6 +231,17 @@
 
     low_lanes = lax.broadcasted_iota(jnp.int32, (BLK, 128), 1) < BLK
     batch = owners // 4
+    chips, chip = owners // 2, me // 2
+    side = math.isqrt(chips)
+
+    def distance(offset):
+        return sum(min(d, side - d) for d in divmod(offset, side))
+
+    ranked = sorted(range(1, chips), key=lambda o: (-distance(o), o % side == 0 or o < side))
+    order = []
+    for begin in range(0, chips - 1, 5):
+        taken = ranked[begin : begin + 5]
+        order.append((begin, len(taken), sum(o * chips**i for i, o in enumerate(taken))))
 
     def one_layer(layer, now, done):
         act, after = (act_even, act_odd)[now], (act_odd, act_even)[now]
@@ -252,20 +264,26 @@
             second = tabs[home, base, owners + q]
             return jnp.where(low_lanes, act[first], act[second])
 
-        def give(d, c):
-            q = lax.rem(me + d, owners)
+        def give(q, number):
             send[now, q] = pair(q)
             pltpu.make_async_remote_copy(
                 src_ref=send.at[now, q], dst_ref=recv.at[me],
-                send_sem=a2a_send.at[now], recv_sem=a2a_recv.at[now, d // batch],
+                send_sem=a2a_send.at[now], recv_sem=a2a_recv.at[now, number // batch],
                 device_id={"neuron": q}, device_id_type=MESH,
             ).start()
-            return c
-
-        lax.fori_loop(1, owners // 2, give, 0)
-
-        done = ring_until(done, jnp.where(layer > 0, begin + steps // 8, 0))
-        lax.fori_loop(owners // 2, owners, give, 0)
+
+        def give_chip(number, packed):
+            offset, packed = lax.rem(packed, chips), packed // chips
+            x = lax.rem(chip // side + offset // side, side)
+            y = lax.rem(chip + offset, side)
+            for core in range(2):
+                q = (x * side + y) * 2 + lax.rem(me + core, 2)
+                give(q, number * 2 + core)
+            return packed
+
+        for begin, many, packed in order:
+            lax.fori_loop(begin, begin + many, give_chip, jnp.int32(packed))
+        give(me + 1 - 2 * lax.rem(me, 2), owners - 2)
         recv[me] = pair(me)
 
         done = ring_until(done, needed(layer))
@@ -300,7 +318,7 @@
         lax.fori_loop(groups // 2, groups, near_group, 0)
         for i in range(4):
             done = feed(done, 4 + i)
-            got = recv.at[pl.ds(0, batch - 1 if i == 0 else batch)]
+            got = recv.at[pl.ds(0, batch - 1 if i == 3 else batch)]
             pltpu.make_async_copy(got, got, a2a_recv.at[now, i]).wait()
 
         def far_group(g, c):

time: 246 us -> 235 us (0.955)
  Pallas kernels: 239 us -> 228 us
    pallas_call x1, Pallas kernels: 239 us -> 228 us  [local(): pl.pallas_call(functools.partial(kernel, dims), out_shape=jax.ShapeDtypeS...]
where the time goes in v3:
time: 235 us
  Pallas kernels  228 us (97%)
  local copies, waits for them, and re-layouts  4.59 us (2%)
    pallas_call x1, Pallas kernels, local(): pl.pallas_call(functools.partial(kernel, dims), out_shape=jax.ShapeDtypeS...  228 us

profile of v3, /device:TPU:1, one launch (start us, length us, event | category | flops | bytes accessed | tf_op | source)
XLA Modules:
  0.0 234.8 jit_solution(9865603230870795490)
XLA Ops:
  0.0 0.0 copy-start
  0.0 0.1 pad.17.clone
  0.1 0.8 convert_bitcast_fusion
  0.9 0.8 reshape.64
  1.7 0.2 select_reduce_fusion
  1.9 0.1 pad_add_fusion.1
  2.0 0.2 select_reduce_fusion.4
  2.2 0.2 select_reduce_fusion.3
  2.4 0.1 pad_add_fusion
  2.5 0.8 copy.11
  3.3 0.1 reshape.65
  3.4 0.1 add_add_fusion
  3.5 0.0 copy-done
  3.5 0.3 copy.10
  3.8 0.0 copy-start.1
  3.8 1.6 copy-done.1
  5.4 228.4 %shard_map.55 = bf16[32,64,128]{2,1,0:T(8,128)(2,1)S(1)} custom-call(bf16[32,64,128]{2,1,0:T(8,128)(2,1)S(1)} %bitcast.28, bf16[2,32,64,256]{3,2,1,0:T(8,128)(2,1)S(1)} %bitcast.27, f32[2,16,128]{2,1,0:T(8,128)S(1)} %bitcast.30, s32[8,128]{1,0:T(8,128)S(1)} %bitcast.31), custom_call_target="tpu_custom_call" | custom-call | tf_op jit(solution)/shard_map/pallas_call | solution.py:389
  233.9 0.9 copy.14
  (10 shorter events, 0.1 us)
Async XLA Ops:
  0.0 3.5 %copy-start = (bf16[4,128,2048]{2,1,0:T(8,128)(2,1)S(1)}, bf16[4,128,2048]{2,1,0:T(8,128)(2,1)}, u32[]{:S(2)}) copy-start(bf16[4,128,2048]{2,1,0:T(8,128)(2,1)} %param.5) | copy-start | bytes 6291460
  3.8 1.6 copy-start.1

commit v4 on v3

--- a/solution.py
+++ b/solution.py
@@ -19,39 +19,34 @@
 GROUP = 16
 
 
-def tables(cols, near, owners, me):
-    layers = cols.shape[0]
-    grid = cols.reshape(layers, owners, -1)
-    per = grid.shape[2]
-    place = lax.broadcasted_iota(jnp.int32, grid.shape, 2)
-    asked = (grid // per) == me
-    first = jnp.min(jnp.where(asked, place, per - 1), axis=2, keepdims=True)
-    last = jnp.max(jnp.where(asked, place, 0), axis=2, keepdims=True)
-    inside = grid % per
-    send = jnp.concatenate(
-        [
-            jnp.sum(jnp.where(place == first, inside, 0), axis=2),
-            jnp.sum(jnp.where(place == last, inside, 0), axis=2),
-        ],
-        axis=1,
-    )
-    mine = lax.dynamic_index_in_dim(grid, me, 1, keepdims=False) // per
-    same = mine[:, :, None] == mine[:, None, :]
-    earlier = lax.broadcasted_iota(jnp.int32, same.shape, 2) < lax.broadcasted_iota(
-        jnp.int32, same.shape, 1
-    )
-    slot = jnp.max(jnp.where(same & earlier, 1, 0), axis=2)
-    row = lambda v: jnp.pad(v, ((0, 0), (0, 128 - v.shape[1])))
-    far = jnp.concatenate([mine, slot], axis=1)
-    packed = jnp.stack(
-        [row(send), row(near.reshape(layers, -1)), row(far), jnp.zeros((layers, 128), jnp.int32)],
-        axis=1,
-    )
-    return packed.reshape(layers * 4, 128)
+def table(cols, per, me, roll):
+    rows = cols.shape[0]
+    many = 128 // per
+    lane = lax.broadcasted_iota(jnp.int32, (rows, 128), 1)
+    row = lax.broadcasted_iota(jnp.int32, (rows, 128), 0)
+    key = lax.rem(lane, per) * per + lax.rem(cols, per)
+    asked = cols // per == me
+    result = jnp.zeros((rows, 128), jnp.int32)
+    for g in range(many):
+        here = asked & (lane // per == g)
+        low = jnp.min(jnp.where(here, key, per * per - 1), axis=1, keepdims=True)
+        high = jnp.max(jnp.where(here, key, 0), axis=1, keepdims=True)
+        result = jnp.where(lane == g, lax.rem(low, per), result)
+        result = jnp.where(lane == many + g, lax.rem(high, per), result)
+    mine = jnp.sum(jnp.where(row == me // many, cols // per, 0), axis=0, keepdims=True)
+    mine = jnp.zeros((rows, 128), jnp.int32) + mine
+    mine = roll(mine, lax.rem(per - per * lax.rem(me, many) + 128, 128))
+    slot = jnp.zeros((rows, 128), jnp.int32)
+    for k in range(1, per):
+        slot = jnp.where((roll(mine, k) == mine) & (lane >= per + k), 1, slot)
+    far = (lane >= per) & (lane < 2 * per)
+    result = jnp.where(far & (row == 3), mine, result)
+    return jnp.where(far & (row == 4), slot, result)
 
 
 def kernel(
-    dims, x_ref, w_ref, b_ref, t_ref, o_ref,
+    dims, x_ref, w_ref, b_ref, near_ref, cols_ref, o_ref,
+    x_in,
     act_even, act_odd, total, send, recv_even, recv_odd, wbuf, ball, btr, tall, tabs,
     local_sem, small_send, small_recv, a2a_send, a2a_recv, ring_send, ring_recv,
 ):
@@ -63,49 +58,33 @@
     behind = lax.rem(s + sections - 1, sections)
     last = sections - 1
 
+    barrier = pltpu.get_barrier_semaphore()
+
+    def greet(d, carry):
+        pl.semaphore_signal(
+            barrier, inc=1, device_id={"neuron": lax.rem(me + d, owners)}, device_id_type=MESH
+        )
+        return carry
+
+    lax.fori_loop(1, owners, greet, 0)
+
+    def greet_section(d, carry):
+        pl.semaphore_signal(
+            barrier, inc=1, device_id={"segment": lax.rem(s + d, sections)}, device_id_type=MESH
+        )
+        return carry
+
+    lax.fori_loop(1, sections, greet_section, 0)
+
+    share_rows = rows // x_in.shape[0]
+    mine = x_ref.at[:, pl.ds(pl.multiple_of(s * share_rows, share_rows), share_rows)]
     loads = [
-        pltpu.make_async_copy(x_ref, act_even, local_sem.at[0]),
+        pltpu.make_async_copy(mine, x_in, local_sem.at[0]),
         pltpu.make_async_copy(w_ref, wbuf.at[pl.ds(s * own, own)], local_sem.at[1]),
     ]
     for load in loads:
         load.start()
-    tall[pl.ds(s, 1)] = t_ref[...][None]
-    ball[pl.ds(s * own, own)] = b_ref[...]
-
-    barrier = pltpu.get_barrier_semaphore()
-
-    def greet(d, carry):
-        pl.semaphore_signal(
-            barrier, inc=1, device_id={"neuron": lax.rem(me + d, owners)}, device_id_type=MESH
-        )
-        return carry
-
-    lax.fori_loop(1, owners, greet, 0)
-
-    def greet_section(d, carry):
-        pl.semaphore_signal(
-            barrier, inc=1, device_id={"segment": lax.rem(s + d, sections)}, device_id_type=MESH
-        )
-        return carry
-
-    lax.fori_loop(1, sections, greet_section, 0)
     pl.semaphore_wait(barrier, owners - 1 + sections - 1)
-
-    def share(d, carry):
-        to = {"segment": lax.rem(s + d, sections)}
-        pltpu.make_async_remote_copy(
-            src_ref=tall.at[pl.ds(s, 1)], dst_ref=tall.at[pl.ds(s, 1)],
-            send_sem=small_send.at[0], recv_sem=small_recv.at[0],
-            device_id=to, device_id_type=MESH,
-        ).start()
-        pltpu.make_async_remote_copy(
-            src_ref=ball.at[pl.ds(s * own, own)], dst_ref=ball.at[pl.ds(s * own, own)],
-            send_sem=small_send.at[1], recv_sem=small_recv.at[1],
-            device_id=to, device_id_type=MESH,
-        ).start()
-        return carry
-
-    lax.fori_loop(1, sections, share, 0)
 
     units = per // UNIT
     first = (FIRST_SHARE, units - FIRST_SHARE)
@@ -114,21 +93,21 @@
     lone = window[0] - SKEW
     end = window[1] * sections
 
-    def ring(source, home, i, side, to, own_source):
+    def ring(home, i, side):
         later = (i >= first[side]).astype(jnp.int32)
         begin = 0 if side == 0 else first[0] + later * (second[0] - first[0])
         place = begin + i - later * first[side]
         at = pl.ds(place * UNIT, UNIT)
         layer = home * own + later
         return pltpu.make_async_remote_copy(
-            src_ref=source.at[later if own_source else layer, at], dst_ref=wbuf.at[layer, at],
+            src_ref=wbuf.at[layer, at], dst_ref=wbuf.at[layer, at],
             send_sem=ring_send.at[side, later], recv_sem=ring_recv.at[side, home, i],
-            device_id={"segment": to}, device_id_type=MESH,
+            device_id={"segment": (ahead, behind)[side]}, device_id_type=MESH,
         )
 
     def hand_on(side, home, i, fine, hops):
         home, i = jnp.clip(home, 0, last), jnp.clip(i, 0, window[side] - 1)
-        copy = ring(wbuf, home, i, side, (ahead, behind)[side], False)
+        copy = ring(home, i, side)
 
         @pl.when(fine)
         def _():
@@ -146,7 +125,7 @@
         @pl.when(fine)
         def _():
             i_in = jnp.clip(i, 0, window[side] - 1)
-            ring(w_ref, s, i_in, side, (ahead, behind)[side], True).start()
+            ring(s, i_in, side).start()
 
     def ring_step(e):
         t = e - own_base
@@ -205,9 +184,62 @@
     def needed(layer):
         return jnp.minimum(LEAD + layer * (end + BEHIND - LEAD) // (layers - 1), end)
 
+    def own_table(t):
+        cols = jnp.concatenate(
+            [cols_ref[t : t + 1, r : r + 128] for r in range(0, cols_ref.shape[1], 128)], axis=0
+        )
+        tall[s * own + t] = table(cols, per, me, lambda v, k: pltpu.roll(v, k, 1))
+        for k in range(3):
+            tall[s * own + t, k : k + 1, per : 2 * per] = near_ref[k, t : t + 1, :]
+        for i in range(per // 2):
+            ball[s * own + t, i : i + 1, :] = b_ref[t : t + 1, i * 128 : (i + 1) * 128].astype(
+                jnp.float32
+            )
+
+    def share(d, carry):
+        to = {"segment": lax.rem(s + d, sections)}
+        pltpu.make_async_remote_copy(
+            src_ref=tall.at[pl.ds(s * own, own)], dst_ref=tall.at[pl.ds(s * own, own)],
+            send_sem=small_send.at[0], recv_sem=small_recv.at[0],
+            device_id=to, device_id_type=MESH,
+        ).start()
+        pltpu.make_async_remote_copy(
+            src_ref=ball.at[pl.ds(s * own, own)], dst_ref=ball.at[pl.ds(s * own, own)],
+            send_sem=small_send.at[1], recv_sem=small_recv.at[1],
+            device_id=to, device_id_type=MESH,
+        ).start()
+        return carry
+
+
+    def bias_columns(i):
+        rows_of = jnp.concatenate(
+            [
+                jnp.zeros((BLK, 128), jnp.float32),
+                ball[:, i, :],
+                jnp.zeros((BLK - layers, 128), jnp.float32),
+            ],
+            axis=0,
+        )
+        btr[2 * i : 2 * i + 2] = rows_of.T.astype(jnp.bfloat16).reshape(2, BLK, 128)
+
+    def take_samples(i):
+        part = x_in[:, :, i * 128 : (i + 1) * 128].reshape(rows, 128).astype(jnp.float32)
+        part = jnp.concatenate([part, part], axis=0).T.astype(jnp.bfloat16)
+        act_even[2 * i : 2 * i + 2] = part.reshape(2, BLK, 128)
+
+    loads[1].wait()
     done = ring_until(0, SKEW)
+    for t in range(own):
+        own_table(t)
+        done = ring_until(done, done + 1)
+    lax.fori_loop(1, sections, share, 0)
+    loads[0].wait()
+    for i in range(per // 2):
+        take_samples(i)
+        if i % 4 == 3:
+            done = ring_until(done, done + 1)
     pltpu.make_async_copy(
-        tall.at[pl.ds(0, sections - 1)], tall.at[pl.ds(0, sections - 1)], small_recv.at[0]
+        tall.at[pl.ds(0, layers - own)], tall.at[pl.ds(0, layers - own)], small_recv.at[0]
     ).wait()
     table_load = pltpu.make_async_copy(tall, tabs, local_sem.at[2])
     table_load.start()
@@ -215,22 +247,14 @@
         ball.at[pl.ds(0, layers - own)], ball.at[pl.ds(0, layers - own)], small_recv.at[1]
     ).wait()
     for i in range(per // 2):
-        rows_of = jnp.concatenate(
-            [
-                jnp.zeros((BLK, 128), jnp.float32),
-                ball[:, i, :],
-                jnp.zeros((BLK - layers, 128), jnp.float32),
-            ],
-            axis=0,
-        )
-        btr[2 * i : 2 * i + 2] = rows_of.T.astype(jnp.bfloat16).reshape(2, BLK, 128)
-    done = ring_until(done, 2 * SKEW)
+        bias_columns(i)
+        if i % 4 == 3:
+            done = ring_until(done, done + 1)
     table_load.wait()
-    for load in loads:
-        load.wait()
 
     low_lanes = lax.broadcasted_iota(jnp.int32, (BLK, 128), 1) < BLK
     batch = owners // 4
+    many = 128 // per
     chips, chip = owners // 2, me // 2
     side = math.isqrt(chips)
 
@@ -246,8 +270,7 @@
     def one_layer(layer, now, done):
         act, after = (act_even, act_odd)[now], (act_odd, act_even)[now]
         recv = (recv_even, recv_odd)[now]
-        home, base = layer // own, lax.rem(layer, own) * 4
-        begin = jnp.maximum(done, needed(layer))
+        begin = begin_steps = jnp.maximum(done, needed(layer))
         steps = jnp.maximum(needed(jnp.minimum(layer + 1, layers - 1)) - begin, 0)
 
         def feed(done, portion):
@@ -260,8 +283,8 @@
             pltpu.make_async_copy(sent, sent, a2a_send.at[now]).wait()
 
         def pair(q):
-            first = tabs[home, base, q]
-            second = tabs[home, base, owners + q]
+            first = tabs[layer, q // many, lax.rem(q, many)]
+            second = tabs[layer, q // many, many + lax.rem(q, many)]
             return jnp.where(low_lanes, act[first], act[second])
 
         def give(q, number):
@@ -281,8 +304,10 @@
                 give(q, number * 2 + core)
             return packed
 
-        for begin, many, packed in order:
-            lax.fori_loop(begin, begin + many, give_chip, jnp.int32(packed))
+        for place, amount, packed in order:
+            lax.fori_loop(place, place + amount, give_chip, jnp.int32(packed))
+            if place == 5:
+                done = ring_until(done, jnp.where(layer > 0, begin_steps + steps // 8, 0))
         give(me + 1 - 2 * lax.rem(me, 2), owners - 2)
         recv[me] = pair(me)
 
@@ -296,7 +321,7 @@
             joined, packed = [], []
             for i in range(GROUP):
                 j = g * GROUP + i
-                near = [act[tabs[home, base + 1, 3 * j + k]] for k in range(3)]
+                near = [act[tabs[layer, k, per + j]] for k in range(3)]
                 joined.append(jnp.concatenate(near + [pick], axis=0))
                 w = wbuf[layer, j]
                 packed.append(
@@ -316,8 +341,8 @@
         lax.fori_loop(0, groups // 2, near_group, 0)
         done = feed(done, 3)
         lax.fori_loop(groups // 2, groups, near_group, 0)
+        done = feed(done, 7)
         for i in range(4):
-            done = feed(done, 4 + i)
             got = recv.at[pl.ds(0, batch - 1 if i == 3 else batch)]
             pltpu.make_async_copy(got, got, a2a_recv.at[now, i]).wait()
 
@@ -325,8 +350,8 @@
             pairs, straights, sums, done = [], [], [], []
             for i in range(GROUP):
                 j = g * GROUP + i
-                pairs.append(recv[tabs[home, base + 2, j]])
-                slot = jnp.zeros((BLK, 128), jnp.int32) + tabs[home, base + 2, per + j]
+                pairs.append(recv[tabs[layer, 3, per + j]])
+                slot = jnp.zeros((BLK, 128), jnp.int32) + tabs[layer, 4, per + j]
                 straights.append(low_lanes == (slot == 0))
             for i in range(GROUP):
                 joined = jnp.concatenate([jnp.zeros((BLK, 128), jnp.bfloat16), pairs[i]], axis=0)
@@ -351,7 +376,11 @@
 
     done = lax.fori_loop(0, layers // 2, two_layers, done)
     ring_until(done, end)
-    o_ref[...] = act_even[...]
+    for i in range(per // 2):
+        part = act_even[2 * i : 2 * i + 2].reshape(128, 128).astype(jnp.float32).T
+        o_ref[:, :, i * 128 : (i + 1) * 128] = (
+            part[:rows].reshape(o_ref.shape[0], -1, 128).astype(jnp.bfloat16)
+        )
 
     for par in range(2):
         sent = send.at[par, pl.ds(0, owners - 1)]
@@ -362,7 +391,7 @@
             count = (first, second)[t][side] * UNIT
             sent = wbuf.at[pl.ds(0, last), pl.ds(0, count)]
             pltpu.make_async_copy(sent, sent, ring_send.at[side, t]).wait()
-    out = tall.at[pl.ds(0, sections - 1)]
+    out = tall.at[pl.ds(0, layers - own)]
     pltpu.make_async_copy(out, out, small_send.at[0]).wait()
     out = ball.at[pl.ds(0, layers - own)]
     pltpu.make_async_copy(out, out, small_send.at[1]).wait()
@@ -372,31 +401,26 @@
     batches, rows, width = samples.shape
     sections = lax.axis_size("segment")
     owners = lax.axis_size("neuron")
-    s = lax.axis_index("segment")
-    me = lax.axis_index("neuron")
     per = width // BLK
     own = weights.shape[0]
     layers = own * sections
     share = rows // sections
     count = batches * share
-    mine = lax.dynamic_slice_in_dim(samples, s * share, share, 1).reshape(count, width)
-    x = mine.T
-    x = jnp.concatenate([x, x], axis=1).reshape(per, BLK, 128)
-    table = tables(remote_cols, near_blocks, owners, me)
-    bias = biases.astype(jnp.float32).reshape(own, width // 128, 128)
     dims = (sections, owners, per, layers, count)
     bf16, f32 = jnp.bfloat16, jnp.float32
-    out = pl.pallas_call(
+    return pl.pallas_call(
         functools.partial(kernel, dims),
-        out_shape=jax.ShapeDtypeStruct((per, BLK, 128), bf16),
+        out_shape=jax.ShapeDtypeStruct((batches, share, width), bf16),
         in_specs=[
-            pl.BlockSpec(memory_space=pl.ANY),
-            pl.BlockSpec(memory_space=pl.ANY),
+            pl.BlockSpec(memory_space=pltpu.HBM),
+            pl.BlockSpec(memory_space=pltpu.HBM),
+            pl.BlockSpec(memory_space=pltpu.VMEM),
             pl.BlockSpec(memory_space=pltpu.VMEM),
             pl.BlockSpec(memory_space=pltpu.VMEM),
         ],
         out_specs=pl.BlockSpec(memory_space=pltpu.VMEM),
         scratch_shapes=[
+            pltpu.VMEM((batches, share, width), bf16),
             pltpu.VMEM((per, BLK, 128), bf16),
             pltpu.VMEM((per, BLK, 128), bf16),
             pltpu.VMEM((per, BLK, 128), f32),
@@ -406,8 +430,8 @@
             pltpu.VMEM((layers, per, BLK, 256), bf16),
             pltpu.VMEM((layers, width // 128, 128), f32),
             pltpu.VMEM((per, BLK, 128), bf16),
-            pltpu.VMEM((sections, own * 4, 128), jnp.int32),
-            pltpu.SMEM((sections, own * 4, 128), jnp.int32),
+            pltpu.VMEM((layers, remote_cols.shape[1] // 128, 128), jnp.int32),
+            pltpu.SMEM((layers, remote_cols.shape[1] // 128, 128), jnp.int32),
             pltpu.SemaphoreType.DMA((3,)),
             pltpu.SemaphoreType.DMA((2,)),
             pltpu.SemaphoreType.DMA((2,)),
@@ -417,11 +441,15 @@
             pltpu.SemaphoreType.DMA((2, sections, own * per // UNIT)),
         ],
         compiler_params=pltpu.CompilerParams(
-            collective_id=0, has_side_effects=True, vmem_limit_bytes=48 * 1024 * 1024
+            collective_id=0, has_side_effects=True, vmem_limit_bytes=62 * 1024 * 1024
         ),
-    )(x, weights.reshape(own, per, BLK, 256), bias, table)
-    y = out.reshape(width, 128)[:, :count].T
-    return y.reshape(batches, share, width)
+    )(
+        samples,
+        weights.reshape(own, per, BLK, 256),
+        biases,
+        near_blocks.transpose(2, 0, 1),
+        remote_cols,
+    )
 
 
 def solution(mesh):

time: 235 us -> 232 us (0.987)
  Pallas kernels: 228 us -> 231 us
  local copies, waits for them, and re-layouts: 4.59 us -> 1.67 us
where the time goes in v4:
time: 232 us
  Pallas kernels  231 us (100%)
    pallas_call x1, Pallas kernels, local(): pl.pallas_call(functools.partial(kernel, dims), out_shape=jax.ShapeDtypeS...  231 us

profile of v4, /device:TPU:1, one launch (start us, length us, event | category | flops | bytes accessed | tf_op | source)
XLA Modules:
  0.0 232.3 jit_solution(11031687108902032347)
XLA Ops:
  0.0 230.6 %shard_map.55 = bf16[4,16,2048]{2,1,0:T(8,128)(2,1)} custom-call(bf16[4,128,2048]{2,1,0:T(8,128)(2,1)} %x_ref.1, bf16[2,32,64,256]{3,2,1,0:T(8,128)(2,1)} %bitcast.2, bf16[2,2048]{1,0:T(2,128)(2,1)} %b_ref.1, s32[3,2,32]{2,1,0:T(2,128)} %bitcast.3, s32[2,1024]{1,0:T(2,128)} %cols_ref.1), custom_call_target="tpu_custom_call" | custom-call | tf_op jit(solution)/shard_map/pallas_call | solution.py:411
  230.6 1.7 copy.7

commit v5 on v4

--- a/solution.py
+++ b/solution.py
@@ -341,7 +341,7 @@
         lax.fori_loop(0, groups // 2, near_group, 0)
         done = feed(done, 3)
         lax.fori_loop(groups // 2, groups, near_group, 0)
-        done = feed(done, 7)
+        done = feed(done, 6)
         for i in range(4):
             got = recv.at[pl.ds(0, batch - 1 if i == 3 else batch)]
             pltpu.make_async_copy(got, got, a2a_recv.at[now, i]).wait()
@@ -366,9 +366,9 @@
             return c
 
         lax.fori_loop(0, groups // 2, far_group, 0)
-        done = feed(done, 8)
+        done = feed(done, 7)
         lax.fori_loop(groups // 2, groups, far_group, 0)
-        return done
+        return feed(done, 8)
 
     def two_layers(i, done):
         done = one_layer(2 * i, 0, done)

time: 232 us -> 231 us (level)
  no operation moved by 1% of the time
where the time goes in v5:
time: 231 us; the launch traced here: 230 us
  Pallas kernels  229 us (99%)
    pallas_call x1, Pallas kernels, local(): pl.pallas_call(functools.partial(kernel, dims), out_shape=jax.ShapeDtypeS...  229 us

profile of v5, /device:TPU:1, one launch (start us, length us, event | category | flops | bytes accessed | tf_op | source)
XLA Modules:
  0.0 230.3 jit_solution(9975456773772251951)
XLA Ops:
  0.0 228.7 %shard_map.55 = bf16[4,16,2048]{2,1,0:T(8,128)(2,1)} custom-call(bf16[4,128,2048]{2,1,0:T(8,128)(2,1)} %x_ref.1, bf16[2,32,64,256]{3,2,1,0:T(8,128)(2,1)} %bitcast.2, bf16[2,2048]{1,0:T(2,128)(2,1)} %b_ref.1, s32[3,2,32]{2,1,0:T(2,128)} %bitcast.3, s32[2,1024]{1,0:T(2,128)} %cols_ref.1), custom_call_target="tpu_custom_call" | custom-call | tf_op jit(solution)/shard_map/pallas_call | solution.py:411
  228.7 1.7 copy.7
